TPU v7x, 32 devices: a whole 2x2x4 slice. The times are simulated.
32 devices in a mesh: dp: 16 (over z, y, x), tensor: 2 (over core).
Axes of the slice: x: 2, y: 2, z: 4, core: 2. Of those that a mesh axis runs over, the one named last changes fastest.
Arguments:
- tokens: bfloat16 [16384, 768], P('dp'), may hold values from -6 to 6
- lengths: int32 [16, 6], P('dp'), may hold values from 1 to 768, 1024 in all within a row
- gene_ids: int32 [16384], P('dp'), may hold values from 0 to 35999
- norm1_gain: float32 [768], replicated, may hold values from 0.5 to 1.5
- norm1_shift: float32 [768], replicated, may hold values from -1.75 to 1.75
- qkv_weight: bfloat16 [768, 3, 768], P(None, None, 'tensor'), may hold values from -0.21875 to 0.21875
- qv_bias: float32 [2, 768], P(None, 'tensor'), may hold values from -1.75 to 1.75
- out_weight: bfloat16 [768, 768], P('tensor'), may hold values from -0.625 to 0.625
- out_bias: float32 [768], replicated, may hold values from -1.75 to 1.75
- norm2_gain: float32 [768], replicated, may hold values from 0.5 to 1.5
- norm2_shift: float32 [768], replicated, may hold values from -1.75 to 1.75
- up_weight: bfloat16 [768, 3072], P(None, 'tensor'), may hold values from -0.21875 to 0.21875
- up_bias: float32 [3072], P('tensor'), may hold values from -1.75 to 1.75
- down_weight: bfloat16 [3072, 768], P('tensor'), may hold values from -0.109375 to 0.109375
- down_bias: float32 [768], replicated, may hold values from -1.75 to 1.75
- cotangent: bfloat16 [16384, 768], P('dp'), may hold values from -6 to 6
Outputs:
- output: bfloat16 [16384, 768], P('dp')
- input_grad: bfloat16 [16384, 768], P('dp')
- norm1_gain_grad: float32 [768], replicated
- norm1_shift_grad: float32 [768], replicated
- qkv_grad: float32 [768, 3, 768], P(None, None, 'tensor')
- qv_bias_grad: float32 [2, 768], P(None, 'tensor')
- out_grad: float32 [768, 768], P('tensor')
- out_bias_grad: float32 [768], replicated
- norm2_gain_grad: float32 [768], replicated
- norm2_shift_grad: float32 [768], replicated
- up_grad: float32 [768, 3072], P(None, 'tensor')
- up_bias_grad: float32 [3072], P('tensor')
- down_grad: float32 [3072, 768], P('tensor')
- down_bias_grad: float32 [768], replicated
- gene_counts: int32 [36000], P('tensor')
Inputs may be any that keep to these rules, and one draw needn't show every extreme that they name: The lengths of one row fill the 1024 token slots of one device.
All inputs are finite; a program needn't handle non-finite values.
Results may differ from a plain program's by a relative error of at most 0.01.
Values sent between devices are 32-bit elements; how exact they have to be, the bound alone decides.
A program may use at most 192 MiB of HBM per device.

v0:
```python
import jax
import jax.numpy as jnp
from jax import lax
from jax.sharding import PartitionSpec as P

HEAD = 64
VOCAB = 36000


def layer_norm(field, norm_gain, norm_shift):
    row_mean = jnp.mean(field, axis=-1, keepdims=True)
    centred = field - row_mean
    variance = jnp.mean(centred * centred, axis=-1, keepdims=True)
    return centred * lax.rsqrt(variance + 1e-05) * norm_gain + norm_shift


def gelu_erf(upper_pre):
    return 0.5 * upper_pre * (1.0 + jax.scipy.special.erf(upper_pre * 0.7071067811865476))


def cell_mask(length_row, tok_rows):
    position = jnp.arange(tok_rows, dtype=jnp.int32)
    cell_ends = jnp.cumsum(length_row)
    segment = jnp.sum((position[:, None] >= cell_ends[None, :]).astype(jnp.int32), axis=1)
    return segment[:, None] == segment[None, :]


def over_rows(left, right):
    return lax.dot_general(
        left, right, (((0,), (0,)), ((), ())), preferred_element_type=jnp.float32
    )


def by_transpose(left, right):
    return lax.dot_general(
        left, right, (((1,), (1,)), ((), ())), preferred_element_type=jnp.float32
    )


def count_genes(gene_ids, vocab_start, vocab_local):
    tok_rows = gene_ids.shape[0]
    block_rows = min(128, tok_rows)
    shifted = (gene_ids - vocab_start).reshape(tok_rows // block_rows, block_rows)
    column_ids = jnp.arange(vocab_local, dtype=jnp.int32)
    ones_row = jnp.ones((1, block_rows), jnp.bfloat16)

    def add_block(counted, block_ids):
        onehot = (block_ids[:, None] == column_ids[None, :]).astype(jnp.bfloat16)
        return (counted + jnp.dot(ones_row, onehot, preferred_element_type=jnp.float32)[0], None)

    counted, unused = lax.scan(add_block, jnp.zeros((vocab_local,), jnp.float32), shifted)
    return counted


def attention_scores(queries, key_rows, same_cell):
    scores = jnp.einsum(
        "qhe,khe->hqk", queries, key_rows, preferred_element_type=jnp.float32
    ) * HEAD ** (-0.5)
    return jnp.where(same_cell[None], scores, -1000000000.0)


def on_device(
    tokens,
    lengths,
    gene_ids,
    norm1_gain,
    norm1_shift,
    qkv_weight,
    qv_bias,
    out_weight,
    out_bias,
    norm2_gain,
    norm2_shift,
    up_weight,
    up_bias,
    down_weight,
    down_bias,
    cotangent,
):
    tok_rows = tokens.shape[0]
    features = tokens.shape[1]
    head_cols = qkv_weight.shape[2]
    local_heads = head_cols // HEAD
    vocab_local = VOCAB // lax.axis_size("tensor")
    gene_total = count_genes(gene_ids, lax.axis_index("tensor") * vocab_local, vocab_local)
    same_cell = cell_mask(lengths[0], tok_rows)
    inputs = tokens.astype(jnp.float32)
    normed1_f, norm1_pull = jax.vjp(layer_norm, inputs, norm1_gain, norm1_shift)
    normed1 = normed1_f.astype(jnp.bfloat16)
    qkv_flat = qkv_weight.reshape(features, 3 * head_cols)
    qkv_all = jnp.dot(normed1, qkv_flat, preferred_element_type=jnp.float32)
    queries = (
        (qkv_all[:, :head_cols] + qv_bias[0])
        .astype(jnp.bfloat16)
        .reshape(tok_rows, local_heads, HEAD)
    )
    key_rows = (
        qkv_all[:, head_cols : 2 * head_cols]
        .astype(jnp.bfloat16)
        .reshape(tok_rows, local_heads, HEAD)
    )
    values = (
        (qkv_all[:, 2 * head_cols :] + qv_bias[1])
        .astype(jnp.bfloat16)
        .reshape(tok_rows, local_heads, HEAD)
    )
    scores = attention_scores(queries, key_rows, same_cell)
    row_peak = jnp.max(scores, axis=-1, keepdims=True)
    exponent = jnp.exp(scores - row_peak)
    row_sum = jnp.sum(exponent, axis=-1, keepdims=True)
    log_total = row_peak + jnp.log(row_sum)
    probs_low = (exponent / row_sum).astype(jnp.bfloat16)
    context = jnp.einsum("hqk,khe->qhe", probs_low, values, preferred_element_type=jnp.float32)
    context = context.astype(jnp.bfloat16).reshape(tok_rows, head_cols)
    attn_terms = jnp.dot(context, out_weight, preferred_element_type=jnp.float32)
    hidden = inputs + lax.psum(attn_terms, "tensor") + out_bias
    normed2_f, norm2_pull = jax.vjp(layer_norm, hidden, norm2_gain, norm2_shift)
    normed2 = normed2_f.astype(jnp.bfloat16)
    upper_pre = jnp.dot(normed2, up_weight, preferred_element_type=jnp.float32) + up_bias
    active_f, gelu_pull = jax.vjp(gelu_erf, upper_pre)
    active = active_f.astype(jnp.bfloat16)
    ffn_terms = jnp.dot(active, down_weight, preferred_element_type=jnp.float32)
    output = (hidden + lax.psum(ffn_terms, "tensor") + down_bias).astype(jnp.bfloat16)
    grad_output = cotangent.astype(jnp.float32)
    down_bias_grad = jnp.sum(grad_output, axis=0)
    down_grad = over_rows(active, cotangent)
    grad_active = by_transpose(cotangent, down_weight)
    grad_upper = gelu_pull(grad_active)[0].astype(jnp.bfloat16)
    up_bias_grad = jnp.sum(grad_upper.astype(jnp.float32), axis=0)
    up_grad = over_rows(normed2, grad_upper)
    grad_normed2 = lax.psum(by_transpose(grad_upper, up_weight), "tensor")
    grad_hidden_norm, norm2_gain_grad, norm2_shift_grad = norm2_pull(grad_normed2)
    grad_hidden = grad_output + grad_hidden_norm
    grad_branch = grad_hidden.astype(jnp.bfloat16)
    out_bias_grad = jnp.sum(grad_branch.astype(jnp.float32), axis=0)
    out_grad = over_rows(context, grad_branch)
    grad_context = (
        by_transpose(grad_branch, out_weight)
        .astype(jnp.bfloat16)
        .reshape(tok_rows, local_heads, HEAD)
    )
    again = attention_scores(queries, key_rows, same_cell)
    probabilities = jnp.exp(again - log_total)
    probs_again = probabilities.astype(jnp.bfloat16)
    grad_values = jnp.einsum(
        "hqk,qhe->khe", probs_again, grad_context, preferred_element_type=jnp.float32
    )
    grad_probs = jnp.einsum(
        "qhe,khe->hqk", grad_context, values, preferred_element_type=jnp.float32
    )
    grad_scores = probabilities * (
        grad_probs - jnp.sum(probabilities * grad_probs, axis=-1, keepdims=True)
    )
    grad_scores = grad_scores.astype(jnp.bfloat16)
    grad_query = jnp.einsum(
        "hqk,khe->qhe", grad_scores, key_rows, preferred_element_type=jnp.float32
    ) * HEAD ** (-0.5)
    grad_keys = jnp.einsum(
        "hqk,qhe->khe", grad_scores, queries, preferred_element_type=jnp.float32
    ) * HEAD ** (-0.5)
    grad_qkv = jnp.concatenate(
        [
            grad_query.reshape(tok_rows, head_cols),
            grad_keys.reshape(tok_rows, head_cols),
            grad_values.reshape(tok_rows, head_cols),
        ],
        axis=1,
    ).astype(jnp.bfloat16)
    grad_qkv_f = grad_qkv.astype(jnp.float32)
    qv_bias_grad = jnp.stack(
        [
            jnp.sum(grad_qkv_f[:, :head_cols], axis=0),
            jnp.sum(grad_qkv_f[:, 2 * head_cols :], axis=0),
        ]
    )
    qkv_grad = over_rows(normed1, grad_qkv).reshape(features, 3, head_cols)
    grad_normed1 = lax.psum(by_transpose(grad_qkv, qkv_flat), "tensor")
    grad_input_norm, norm1_gain_grad, norm1_shift_grad = norm1_pull(grad_normed1)
    input_grad = (grad_hidden + grad_input_norm).astype(jnp.bfloat16)
    (
        norm1_gain_grad,
        norm1_shift_grad,
        qkv_grad,
        qv_bias_grad,
        out_grad,
        out_bias_grad,
        norm2_gain_grad,
        norm2_shift_grad,
        up_grad,
        up_bias_grad,
        down_grad,
        down_bias_grad,
        gene_total,
    ) = lax.psum(
        (
            norm1_gain_grad,
            norm1_shift_grad,
            qkv_grad,
            qv_bias_grad,
            out_grad,
            out_bias_grad,
            norm2_gain_grad,
            norm2_shift_grad,
            up_grad,
            up_bias_grad,
            down_grad,
            down_bias_grad,
            gene_total,
        ),
        "dp",
    )
    gene_counts = gene_total.astype(jnp.int32)
    return (
        output,
        input_grad,
        norm1_gain_grad,
        norm1_shift_grad,
        qkv_grad,
        qv_bias_grad,
        out_grad,
        out_bias_grad,
        norm2_gain_grad,
        norm2_shift_grad,
        up_grad,
        up_bias_grad,
        down_grad,
        down_bias_grad,
        gene_counts,
    )


def solution(mesh):
    return jax.shard_map(
        on_device,
        mesh=mesh,
        in_specs=(
            P("dp", None),
            P("dp", None),
            P("dp"),
            P(),
            P(),
            P(None, None, "tensor"),
            P(None, "tensor"),
            P("tensor", None),
            P(),
            P(),
            P(),
            P(None, "tensor"),
            P("tensor"),
            P("tensor", None),
            P(),
            P("dp", None),
        ),
        out_specs=(
            P("dp", None),
            P("dp", None),
            P(),
            P(),
            P(None, None, "tensor"),
            P(None, "tensor"),
            P("tensor", None),
            P(),
            P(),
            P(),
            P(None, "tensor"),
            P("tensor"),
            P("tensor", None),
            P(),
            P("tensor"),
        ),
        check_vma=False,
    )
```

profile of v0, /device:TPU:0, one launch (start us, length us, event | category | flops | bytes accessed | tf_op | source)
XLA Modules:
  0.0 685.7 jit_solution(12716486066576785531)
XLA Ops:
  15.6 4.4 fusion.38
  30.4 11.9 %fusion.48 = (f32[6,1024]{1,0:T(8,128)S(1)}, f32[6,1024,1024]{1,2,0:T(8,128)}) fusion(bf16[1024,6,64]{0,2,1:T(8,128)(2,1)S(1)} %bitcast.54, bf16[1024,6,64]{0,2,1:T(8,128)(2,1)} %bitcast.56, pred[1024,1024]{0,1:T(8,128)(4,1)} %broadcast_compare_fusion), kind=kOutput, calls=%fused_computation.92 | convolution fusion | flops 824174592 | bytes 27811840 | tf_op jit(solution)/shard_map/qhe,khe->hqk/dot_general | solution.py:56
  42.2 10.3 %fusion.7 = f32[6,1024]{1,0:T(8,128)S(1)} fusion(f32[6,1024,1024]{1,2,0:T(8,128)} %get-tuple-element.128, f32[6,1024]{1,0:T(8,128)S(1)} %get-tuple-element.127), kind=kLoop, calls=%fused_computation.15 | loop fusion | flops 12576768 | bytes 25214976 | tf_op jit(solution)/shard_map/reduce_sum | solution.py:110
  52.5 10.6 %fusion.31 = bf16[6,64,1024]{2,1,0:T(8,128)(2,1)S(1)} fusion(bf16[1024,6,64]{0,2,1:T(8,128)(2,1)S(1)} %bitcast.73, f32[6,1024,1024]{1,2,0:T(8,128)} %get-tuple-element.128, f32[6,1024]{1,0:T(8,128)S(1)} %fusion.7, f32[6,1024]{1,0:T(8,128)S(1)} %get-tuple-element.127), kind=kOutput, calls=%fused_computation.64 | convolution fusion | flops 824573952 | bytes 26787840 | tf_op jit(solution)/shard_map/hqk,khe->qhe/dot_general | solution.py:113
  66.7 9.8 %all-reduce.10.cloned.1.call-start = ((), (), s32[]{:S(2)}) async-start(), calls=%async_computation.1 | async-start | bytes 6291456 | tf_op jit(solution)/shard_map/psum | solution.py:131
  76.6 16.2 %all-reduce.8.cloned.1.call-done = f32[1024,768]{1,0:T(8,128)} async-done(((f32[1024,768]{1,0:T(8,128)}), f32[1024,768]{1,0:T(8,128)}) %all-reduce.8.cloned.1.call-update) | async-done | bytes 3145744 | tf_op jit(solution)/shard_map/psum | solution.py:116
  101.3 7.5 %convert_reduce_fusion = (f32[1536]{0:T(1024)S(1)}, bf16[1024,1536]{1,0:T(8,128)(2,1)S(1)}, bf16[1024,1536]{1,0:T(8,128)(2,1)}) fusion(f32[1024,1536]{1,0:T(8,128)S(1)} %fusion.42, f32[1536]{0:T(1024)S(1)} %copy-done.43, bf16[1024,768]{1,0:T(8,128)(2,1)S(1)} %copy-done.12, bf16[1536,768]{1,0:T(8,128)(2,1)S(1)} %copy-done), kind=kOutput, calls=%fused_computation.20 | convolution fusion | flops 2444229120 | bytes 16527360 | tf_op jit(solution)/shard_map/dot_general | solution.py:35
  110.4 4.3 fusion.51
  115.4 6.2 fusion.50
  121.5 17.7 %all-reduce.10.cloned.1.call-done = f32[1024,768]{1,0:T(8,128)} async-done(((f32[1024,768]{1,0:T(8,128)}), f32[1024,768]{1,0:T(8,128)}) %all-reduce.10.cloned.1.call-update) | async-done | bytes 3145744 | tf_op jit(solution)/shard_map/psum | solution.py:131
  149.0 16.2 %multiply_reduce_fusion = (f32[6,1024]{1,0:T(8,128)S(1)}, f32[6,1024,1024]{1,2,0:T(8,128)}) fusion(f32[6,1024,1024]{1,2,0:T(8,128)} %get-tuple-element.128, f32[6,1024]{1,0:T(8,128)S(1)} %log_add_fusion, bf16[1024,6,64]{0,2,1:T(8,128)(2,1)S(1)} %bitcast.70, bf16[1024,6,64]{0,2,1:T(8,128)(2,1)} %bitcast.72), kind=kOutput, calls=%fused_computation.10 | convolution fusion | flops 824174592 | bytes 51953664 | tf_op jit(solution)/shard_map/qhe,khe->hqk/dot_general | solution.py:148
  165.2 17.3 %multiply_convert_fusion = bf16[6,1024,1024]{1,2,0:T(8,128)(2,1)S(1)} fusion(f32[6,1024,1024]{1,2,0:T(8,128)} %get-tuple-element.130, f32[6,1024,1024]{1,2,0:T(8,128)} %get-tuple-element.128, f32[6,1024]{1,0:T(8,128)S(1)} %get-tuple-element.129, f32[6,1024]{1,0:T(8,128)S(1)} %log_add_fusion), kind=kLoop, calls=%fused_computation.9 | loop fusion | flops 25165824 | bytes 62963712 | tf_op jit(solution)/shard_map/convert_element_type | solution.py:154
  182.5 4.6 copy-done.2
  190.3 9.4 %multiply_convert_fusion.2 = bf16[6,64,1024]{2,1,0:T(8,128)(2,1)} fusion(bf16[1024,6,64]{0,2,1:T(8,128)(2,1)S(1)} %bitcast.55, bf16[6,1024,1024]{1,2,0:T(8,128)(2,1)} %copy-done.2), kind=kOutput, calls=%fused_computation.60 | convolution fusion | flops 806092800 | bytes 14155776 | tf_op jit(solution)/shard_map/hqk,qhe->khe/dot_general | solution.py:158
  199.6 12.4 %fusion.28 = bf16[6,64,1024]{2,1,0:T(8,128)(2,1)S(1)} fusion(bf16[1024,6,64]{0,2,1:T(8,128)(2,1)} %bitcast.71, f32[6,1024,1024]{1,2,0:T(8,128)} %get-tuple-element.128, f32[6,1024]{1,0:T(8,128)S(1)} %log_add_fusion), kind=kOutput, calls=%fused_computation.63 | convolution fusion | flops 818282496 | bytes 26763264 | tf_op jit(solution)/shard_map/hqk,qhe->khe/dot_general | solution.py:145
  212.1 5.7 fusion.36
  217.8 14.0 %while.11 = (s32[]{:T(128)}, f32[18000]{0:T(1024)S(1)}, s32[8,128]{1,0:T(8,128)S(1)}, s32[]{:T(128)}, s32[]{:T(128)}) while((s32[]{:T(128)}, f32[18000]{0:T(1024)S(1)}, s32[8,128]{1,0:T(8,128)S(1)}, s32[]{:T(128)}, s32[]{:T(128)}) %tuple.43), condition=%wide.region_39.40_spmd.clone, body=%wide.region_38.39_spmd.clone.sunk | while | flops 6948003 | bytes 289611 | solution.py:51
  231.9 7.1 %fusion.53 = f32[1536,768]{1,0:T(8,128)} fusion(bf16[1024,1536]{1,0:T(8,128)(2,1)} %get-tuple-element.122, bf16[1024,768]{1,0:T(8,128)(2,1)S(1)} %copy-done.13), kind=kOutput, calls=%fused_computation.97 | convolution fusion | flops 2415919104 | bytes 9437184 | tf_op jit(solution)/shard_map/dot_general | solution.py:29
  239.0 4.6 fusion.41
  260.0 81.9 %all-reduce = (f32[768]{0:T(1024)}, f32[768]{0:T(1024)}, f32[2,384]{1,0:T(2,128)}, f32[768]{0:T(1024)}, f32[768]{0:T(1024)}, /*index=5*/f32[768]{0:T(1024)}, f32[1536]{0:T(1024)}, f32[768]{0:T(1024)}) all-reduce(f32[768]{0:T(1024)S(1)} %get-tuple-element.84, ...), channel_id=1, replica_groups=mesh['dp'=16,'tensor'=2] {'dp'}, use_global_device_ids=true, to_apply=%region_18.19 | all-reduce | flops 6912 | bytes 55296 | tf_op jit(solution)/shard_map/psum | solution.py:194
  342.0 4.7 add_convert_fusion.2
  346.6 317.7 %all-reduce.12.cloned.1.call-done = (f32[768,3,384]{0,2,1:T(8,128)}, f32[384,768]{1,0:T(8,128)}, f32[768,1536]{1,0:T(8,128)}, f32[1536,768]{1,0:T(8,128)}, f32[18000]{0:T(1024)}) async-done(((f32[768,3,384]{0,2,1:T(8,128)}, f32[384,768]{1,0:T(8,128)}, f32[768,1536]{1,0:T(8,128)}, f32[1536,768]{1,0:T(8,128)}, f32[18000]{0:T(1024)}), (f32[768,3,384]{0,2,1:T(8,128)}, f32[384,768]{1,0:T(8,128)}, ...) | async-done | bytes 14227792 | tf_op jit(solution)/shard_map/psum | solution.py:194
  664.3 5.3 copy.61
  671.3 5.5 copy.83
  (181 shorter events, 79.6 us)
Async XLA Ops:
  7.2 94.1 %copy-start = (bf16[1536,768]{1,0:T(8,128)(2,1)S(1)}, bf16[1536,768]{1,0:T(8,128)(2,1)}, u32[]{:S(2)}) copy-start(bf16[1536,768]{1,0:T(8,128)(2,1)} %param.31) | copy-start | bytes 7077892
  7.2 8.4 %copy-start.41 = (f32[2,384]{1,0:T(2,128)S(1)}, f32[2,384]{1,0:T(2,128)}, u32[]{:S(2)}) copy-start(f32[2,384]{1,0:T(2,128)} %param.24) | copy-start | bytes 9220
  7.2 8.4 %copy-start.31 = (f32[768]{0:T(1024)S(1)}, f32[768]{0:T(1024)}, u32[]{:S(2)}) copy-start(f32[768]{0:T(1024)} %param.21) | copy-start | bytes 9220
  7.2 8.4 %copy-start.45 = (f32[768]{0:T(1024)S(1)}, f32[768]{0:T(1024)}, u32[]{:S(2)}) copy-start(f32[768]{0:T(1024)} %param.22) | copy-start | bytes 9220
  7.2 85.6 %all-reduce.8.cloned.1.call-start = ((), (), s32[]{:S(2)}) async-start(), calls=%async_computation | async-start | bytes 6291456 | tf_op jit(solution)/shard_map/psum | solution.py:116
  9.1 11.0 %copy-start.28 = (f32[1024]{0:T(1024)}, f32[1024]{0:T(1024)S(1)}, u32[]{:S(2)}) copy-start(f32[1024]{0:T(1024)S(1)} %broadcast_multiply_fusion.1) | copy-start | bytes 12292
  11.7 8.3 %copy-start.33 = (f32[1024]{0:T(1024)}, f32[1024]{0:T(1024)S(1)}, u32[]{:S(2)}) copy-start(f32[1024]{0:T(1024)S(1)} %fusion.32) | copy-start | bytes 12292
  42.2 10.3 %copy-start.19 = (bf16[1024,384]{0,1:T(8,128)(2,1)S(1)}, bf16[1024,384]{0,1:T(8,128)(2,1)}, u32[]{:S(2)}) copy-start(bf16[1024,384]{0,1:T(8,128)(2,1)} %copy.53) | copy-start | bytes 2359300
  52.5 11.5 %copy-start.26 = (bf16[384,768]{1,0:T(8,128)(2,1)S(1)}, bf16[384,768]{1,0:T(8,128)(2,1)}, u32[]{:S(2)}) copy-start(bf16[384,768]{1,0:T(8,128)(2,1)} %param.25) | copy-start | bytes 1769476
  64.0 28.8 %copy-start.39 = (f32[768]{0:T(1024)S(1)}, f32[768]{0:T(1024)}, u32[]{:S(2)}) copy-start(f32[768]{0:T(1024)} %param.26) | copy-start | bytes 9220
  66.7 72.5 %all-reduce.10.cloned.1.call-start = ((), (), s32[]{:S(2)}) async-start(), calls=%async_computation.1 | async-start | bytes 6291456 | tf_op jit(solution)/shard_map/psum | solution.py:131
  114.7 137.5 %all-reduce.14.cloned.1.call-start = ((), (), s32[]{:S(2)}) async-start(), calls=%async_computation.3 | async-start | bytes 12582912 | tf_op jit(solution)/shard_map/psum | solution.py:123
  149.0 16.2 %copy-start.18 = (bf16[1024,384]{0,1:T(8,128)(2,1)}, bf16[1024,384]{0,1:T(8,128)(2,1)S(1)}, u32[]{:S(2)}) copy-start(bf16[1024,384]{0,1:T(8,128)(2,1)S(1)} %convolution_convert_fusion) | copy-start | bytes 2359300
  165.2 21.9 %copy-start.11 = (bf16[1024,384]{0,1:T(8,128)(2,1)S(1)}, bf16[1024,384]{0,1:T(8,128)(2,1)}, u32[]{:S(2)}) copy-start(bf16[1024,384]{0,1:T(8,128)(2,1)} %copy.55) | copy-start | bytes 2359300
  199.6 12.4 %copy-start.15 = (bf16[6,64,1024]{2,1,0:T(8,128)(2,1)S(1)}, bf16[6,64,1024]{2,1,0:T(8,128)(2,1)}, u32[]{:S(2)}) copy-start(bf16[6,64,1024]{2,1,0:T(8,128)(2,1)} %multiply_convert_fusion.3) | copy-start | bytes 2359300
  217.8 446.6 %all-reduce.12.cloned.1.call-start = ((), (), s32[]{:S(2)}) async-start(), calls=%async_computation.2 | async-start | bytes 28459008 | tf_op jit(solution)/shard_map/psum | solution.py:194
  231.8 7.1 %copy-start.20 = (f32[18000]{0:T(1024)}, f32[18000]{0:T(1024)S(1)}, u32[]{:S(2)}) copy-start(f32[18000]{0:T(1024)S(1)} %get-tuple-element.37) | copy-start | bytes 216004
  231.8 7.1 %copy-start.5 = (f32[1024,768]{1,0:T(8,128)S(1)}, f32[1024,768]{1,0:T(8,128)}, u32[]{:S(2)}) copy-start(f32[1024,768]{1,0:T(8,128)} %copy-done.3) | copy-start | bytes 9437188
  231.8 7.1 %copy-start.49 = (bf16[1024,1536]{1,0:T(8,128)(2,1)S(1)}, bf16[1024,1536]{1,0:T(8,128)(2,1)}, u32[]{:S(2)}) copy-start(bf16[1024,1536]{1,0:T(8,128)(2,1)} %copy-done.48) | copy-start | bytes 9437188
  257.5 84.5 %copy-start.38 = (f32[768]{0:T(1024)S(1)}, f32[768]{0:T(1024)}, u32[]{:S(2)}) copy-start(f32[768]{0:T(1024)} %param.32) | copy-start | bytes 9220
  664.3 5.9 copy-start.23
  670.2 6.5 slice-start
  671.3 5.5 slice-start.1
  671.3 7.7 %copy-start.1 = (bf16[1536,768]{1,0:T(8,128)(2,1)S(1)}, bf16[1536,768]{1,0:T(8,128)(2,1)}, u32[]{:S(2)}) copy-start(bf16[1536,768]{1,0:T(8,128)(2,1)} %param.31) | copy-start | bytes 7077892
  (32 other events, 84.1 us)
Sparse Core Ops, SparseCore 0:
  66.8 25.9 all-reduce.7
  114.8 24.3 all-reduce.9
  217.9 33.3 all-reduce.13
  259.9 404.4 all-reduce.11
where the time goes:
time: 694 us; the launch traced here: 686 us
  waiting for transfers between devices  352 us (51%)
  matrix products  129 us (19%)
  blocking collectives  81.9 us (12%)
  other arithmetic  58.4 us (8%)
  local copies, waits for them, and re-layouts  39.8 us (6%)
  between operations  14.5 us (2%)
  starting transfers between devices  9.96 us (1%)
    psum x1, waiting for transfers between devices, on_device(): lax.psum((norm1_gain_grad, norm1_shift_grad, qkv_grad, qv_bias_grad, out_...  318 us
    psum x1, blocking collectives, on_device(): lax.psum((norm1_gain_grad, norm1_shift_grad, qkv_grad, qv_bias_grad, out_...  81.9 us
    unnamed x109, local copies, waits for them, and re-layouts  32.8 us
    dot_general x4, matrix products, by_transpose(): lax.dot_general(left, right, (((1,), (1,)), ((), ())), preferred_element_...  18.3 us
    psum x1, waiting for transfers between devices, on_device(): grad_normed2 = lax.psum(by_transpose(grad_upper, up_weight), 'tensor')  17.7 us
    dot_general x4, matrix products, over_rows(): lax.dot_general(left, right, (((0,), (0,)), ((), ())), preferred_element_...  17.6 us
    convert_element_type x1, other arithmetic, on_device(): grad_scores = grad_scores.astype(jnp.bfloat16)  17.3 us
    psum x1, waiting for transfers between devices, on_device(): hidden = inputs + lax.psum(attn_terms, 'tensor') + out_bias  16.2 us
  transfers between devices with their start and end apart: 4, of which 3 were waited for; matrix products, arithmetic and copies ran while one was open for 7% of the time, Pallas kernels for 0%

commit v1 on v0

--- a/solution.py
+++ b/solution.py
@@ -1,10 +1,161 @@
+import functools
+
 import jax
 import jax.numpy as jnp
 from jax import lax
+from jax.experimental import pallas as pl
+from jax.experimental.pallas import tpu as pltpu
 from jax.sharding import PartitionSpec as P
 
 HEAD = 64
 VOCAB = 36000
+MESH = pl.DeviceIdType.MESH
+
+
+def bit_of(dp, m):
+    return lax.rem(lax.div(dp, m), 2)
+
+class Engine:
+    def __init__(self, n_dp, rows, n_chunks, g, r, o, ssem, rsem, osem):
+        self.g, self.r, self.o, self.ssem, self.rsem, self.osem = g, r, o, ssem, rsem, osem
+        self.bits = n_dp.bit_length() - 1
+        self.half = min(self.bits, 4)
+        self.rows = rows
+        self.n = n_chunks
+        self.dp = lax.axis_index("dp"); self.t = lax.axis_index("tensor")
+        self.flat = self.bits - self.half
+        self.stages = 2 * self.half + self.flat
+
+    def order(self, c, p, k):
+        if p == 0: o = [0, 1, 2]
+        elif p == 1: o = [1, 0, 2]
+        else: o = [2, None, None]
+        if self.bits < 3: return 1 << k
+        if k >= 3: return 1 << k
+        if o[k] is not None: return 1 << o[k]
+        odd = lax.rem(c, 2)
+        return 1 + odd if k == 1 else 2 - odd
+
+    def region(self, c, p, depth):
+        off = 0
+        for k in range(depth):
+            off = off + bit_of(self.dp, self.order(c, p, k)) * (self.rows >> (k + 1))
+        return off
+
+    def copy(self, c, p, s):
+        g, r, rows, H = self.g, self.r, self.rows, self.half
+        if s < H:
+            k = s; h = rows >> (s + 1)
+            m = self.order(c, p, k); b = bit_of(self.dp, m)
+            src = g.at[c, p, pl.ds(pl.multiple_of(self.region(c, p, k) + (1 - b) * h, 8), h)]
+            base = rows - (rows >> s)
+            dst = r.at[c, p, pl.ds(base, h)]
+        elif s < H + self.flat:
+            k = s; h = rows >> H
+            m = self.order(c, p, k); b = bit_of(self.dp, m)
+            src = g.at[c, p, pl.ds(pl.multiple_of(self.region(c, p, H), 8), h)]
+            dst = r.at[c, p, pl.ds(rows - h + (s - H) * h, h)]
+        else:
+            k = self.stages - 1 - s; h = rows >> (k + 1)
+            m = self.order(c, p, k); b = bit_of(self.dp, m)
+            at = pl.ds(pl.multiple_of(self.region(c, p, k + 1), 8), h)
+            dst = self.o.at[c, p, at]; src = g.at[c, p, at] if s == self.stages - self.half else dst
+        partner = self.dp + m * (1 - 2 * b)
+        return pltpu.make_async_remote_copy(src, dst, self.ssem.at[c, p, s], self.rsem.at[c, p, s],
+                                            device_id=(partner, self.t), device_id_type=MESH)
+
+    def add(self, c, p, s):
+        g, r, rows, H = self.g, self.r, self.rows, self.half
+        if s < H:
+            h = rows >> (s + 1); base = rows - (rows >> s)
+            at = pl.ds(pl.multiple_of(self.region(c, p, s + 1), 8), h)
+        elif s < H + self.flat:
+            h = rows >> H; base = rows - h + (s - H) * h
+            at = pl.ds(pl.multiple_of(self.region(c, p, H), 8), h)
+        else:
+            return
+        g[c, p, at] = g[c, p, at] + r[c, p, pl.ds(base, h)]
+
+    def keep(self, c, p):
+        at = pl.ds(pl.multiple_of(self.region(c, p, self.half), 8), self.rows >> self.half)
+        return pltpu.make_async_copy(self.g.at[c, p, at], self.o.at[c, p, at], self.osem.at[c, p])
+
+    def tick(self, tau, parts, done=None):
+        for s in range(self.stages + 1):
+            c = tau - s
+            @pl.when((c >= 0) & (c < self.n))
+            def _():
+                if s > 0:
+                    for p in range(parts):
+                        self.copy(c, p, s - 1).wait()
+                        self.add(c, p, s - 1)
+                        if s == self.stages - self.half:
+                            self.keep(c, p).start()
+                        if s == self.stages - self.half + 1:
+                            self.keep(c, p).wait()
+                        if s < self.stages:
+                            self.copy(c, p, s).start()
+                else:
+                    for p in range(parts):
+                        self.copy(c, p, s).start()
+                if s == self.stages and done is not None:
+                    done(c)
+
+    def r_rows(self):
+        return self.rows - (self.rows >> self.half) + self.flat * (self.rows >> self.half)
+
+def barrier(n_dp, with_core=True):
+    dp = lax.axis_index("dp"); t = lax.axis_index("tensor")
+    bar = pltpu.get_barrier_semaphore()
+    n = 0
+    for k in range(n_dp.bit_length() - 1):
+        m = 1 << k
+        b = bit_of(dp, m)
+        pl.semaphore_signal(bar, inc=1, device_id=(dp + m * (1 - 2 * b), t), device_id_type=MESH); n += 1
+    pl.semaphore_wait(bar, n)
+
+def kern(n_dp, n_chunks, rows, parts, x, o, g, r, ssem, rsem, lsem, osem):
+    ld = pltpu.make_async_copy(x, g, lsem); ld.start()
+    barrier(n_dp)
+    ld.wait()
+    e = Engine(n_dp, rows, n_chunks, g, r, o, ssem, rsem, osem)
+    def body(tau, carry):
+        e.tick(tau, parts); return carry
+    lax.fori_loop(0, n_chunks + e.stages, body, 0)
+
+def allreduce(n_dp, n_chunks=18, rows=256, parts=3, cols=256):
+    bits = n_dp.bit_length()-1; half=min(bits,4); stages = 2*half + bits-half
+    rr = rows - (rows >> half) + (bits-half) * (rows >> half)
+    def f(x):
+        return pl.pallas_call(functools.partial(kern, n_dp, n_chunks, rows, parts),
+            out_shape=jax.ShapeDtypeStruct((n_chunks, parts, rows, cols), jnp.float32),
+            in_specs=[pl.BlockSpec(memory_space=pl.ANY)],
+            out_specs=pl.BlockSpec(memory_space=pl.ANY),
+            scratch_shapes=[pltpu.VMEM((n_chunks, parts, rows, cols), jnp.float32), pltpu.VMEM((n_chunks, parts, rr, cols), jnp.float32),
+              pltpu.SemaphoreType.DMA((n_chunks, parts, stages)), pltpu.SemaphoreType.DMA((n_chunks, parts, stages)), pltpu.SemaphoreType.DMA, pltpu.SemaphoreType.DMA((n_chunks, parts))],
+            compiler_params=pltpu.CompilerParams(collective_id=0, has_side_effects=True, vmem_limit_bytes=60<<20),
+        )(x)
+    return f
+
+
+def pack(down, up, out, qkv):
+    return jnp.concatenate(
+        [
+            down.reshape(6, 256, 3, 256).transpose(0, 2, 1, 3),
+            up.reshape(3, 256, 6, 256).transpose(2, 0, 1, 3),
+            jnp.concatenate([out.reshape(-1), qkv.reshape(-1)]).reshape(6, 3, 256, 256),
+        ]
+    )
+
+
+def unpack(packed, down, up, out, qkv):
+    rest = packed[12:].reshape(-1)
+    return (
+        packed[:6].transpose(0, 2, 1, 3).reshape(down.shape),
+        packed[6:12].transpose(1, 2, 0, 3).reshape(up.shape),
+        rest[: out.size].reshape(out.shape),
+        rest[out.size :].reshape(qkv.shape),
+    )
 
 
 def layer_norm(field, norm_gain, norm_shift):
@@ -177,33 +328,28 @@
     grad_normed1 = lax.psum(by_transpose(grad_qkv, qkv_flat), "tensor")
     grad_input_norm, norm1_gain_grad, norm1_shift_grad = norm1_pull(grad_normed1)
     input_grad = (grad_hidden + grad_input_norm).astype(jnp.bfloat16)
+    packed = pack(down_grad, up_grad, out_grad, qkv_grad)
+    packed = allreduce(lax.axis_size("dp"), packed.shape[0])(packed)
+    down_grad, up_grad, out_grad, qkv_grad = unpack(packed, down_grad, up_grad, out_grad, qkv_grad)
     (
         norm1_gain_grad,
         norm1_shift_grad,
-        qkv_grad,
         qv_bias_grad,
-        out_grad,
         out_bias_grad,
         norm2_gain_grad,
         norm2_shift_grad,
-        up_grad,
         up_bias_grad,
-        down_grad,
         down_bias_grad,
         gene_total,
     ) = lax.psum(
         (
             norm1_gain_grad,
             norm1_shift_grad,
-            qkv_grad,
             qv_bias_grad,
-            out_grad,
             out_bias_grad,
             norm2_gain_grad,
             norm2_shift_grad,
-            up_grad,
             up_bias_grad,
-            down_grad,
             down_bias_grad,
             gene_total,
         ),

time: 694 us -> 720 us (1.037)
  waiting for transfers between devices: 352 us -> 100 us
  Pallas kernels: 0 us -> 211 us
  local copies, waits for them, and re-layouts: 39.8 us -> 111 us
  other arithmetic: 58.4 us -> 70.9 us
  starting transfers between devices: 9.96 us -> 0.38 us
  blocking collectives: 81.9 us -> 74.4 us
    psum x1, waiting for transfers between devices: 318 us -> 88.7 us  [on_device(): lax.psum((norm1_gain_grad, norm1_shift_grad, qv_bias_grad, out_bias_grad,...]
    pallas_call x0 -> x1, Pallas kernels: none -> 211 us  [f(): pl.pallas_call(functools.partial(kern, n_dp, n_chunks, rows, parts), out_...]
    reshape x0 -> x6, local copies, waits for them, and re-layouts: none -> 35.1 us  [the longest x2 14.2 us: pack(): up.reshape(3, 256, 6, 256).transpose(2, 0, 1, 3)]
    slice x0 -> x5, local copies, waits for them, and re-layouts: none -> 19.2 us  [the longest x3 10.3 us: unpack(): rest[out.size:].reshape(qkv.shape)]
    psum x1, waiting for transfers between devices: 17.7 us -> 0.01 us  [on_device(): grad_normed2 = lax.psum(by_transpose(grad_upper, up_weight), 'tensor')]
    concatenate x0 -> x2, other arithmetic: none -> 14.9 us  [the longest x1 10.9 us: pack(): jnp.concatenate([down.reshape(6, 256, 3, 256).transpose(0, 2, 1, 3), up.r...]
    transpose x0 -> x2, local copies, waits for them, and re-layouts: none -> 13.4 us  [the longest x1 10.7 us: unpack(): packed[:6].transpose(0, 2, 1, 3).reshape(down.shape)]
    psum x1, starting transfers between devices: 9.84 us -> 0.04 us  [on_device(): grad_normed2 = lax.psum(by_transpose(grad_upper, up_weight), 'tensor')]
  transfers between devices with their start and end apart: 4 -> 4, of which waited for: 3 -> 2; matrix products, arithmetic and copies ran while one was open for 7% -> 20% of each run, Pallas kernels for 0% -> 30%
where the time goes in v1:
time: 720 us; the launch traced here: 710 us
  Pallas kernels  211 us (29%)
  matrix products  128 us (18%)
  local copies, waits for them, and re-layouts  111 us (15%)
  waiting for transfers between devices  100 us (14%)
  blocking collectives  74.4 us (10%)
  other arithmetic  70.9 us (10%)
  between operations  15.2 us (2%)
    pallas_call x1, Pallas kernels, f(): pl.pallas_call(functools.partial(kern, n_dp, n_chunks, rows, parts), out_...  211 us
    psum x1, waiting for transfers between devices, on_device(): lax.psum((norm1_gain_grad, norm1_shift_grad, qv_bias_grad, out_bias_grad,...  88.7 us
    psum x1, blocking collectives, on_device(): lax.psum((norm1_gain_grad, norm1_shift_grad, qv_bias_grad, out_bias_grad,...  74.4 us
    unnamed x127, local copies, waits for them, and re-layouts  31.1 us
    dot_general x4, matrix products, over_rows(): lax.dot_general(left, right, (((0,), (0,)), ((), ())), preferred_element_...  20.7 us
    dot_general x4, matrix products, by_transpose(): lax.dot_general(left, right, (((1,), (1,)), ((), ())), preferred_element_...  17.2 us
    convert_element_type x1, other arithmetic, on_device(): grad_scores = grad_scores.astype(jnp.bfloat16)  17.1 us
    dot_general x1, matrix products, on_device(): jnp.einsum('qhe,khe->hqk', grad_context, values, preferred_element_type=j...  15.8 us
  transfers between devices with their start and end apart: 4, of which 2 were waited for; matrix products, arithmetic and copies ran while one was open for 20% of the time, Pallas kernels for 30%

profile of v1, /device:TPU:0, one launch (start us, length us, event | category | flops | bytes accessed | tf_op | source)
XLA Modules:
  0.0 710.3 jit_solution(18358832808970163423)
XLA Ops:
  30.7 11.9 %fusion.48 = (f32[6,1024]{1,0:T(8,128)S(1)}, f32[6,1024,1024]{1,2,0:T(8,128)}) fusion(bf16[1024,6,64]{0,2,1:T(8,128)(2,1)S(1)} %bitcast.81, bf16[1024,6,64]{0,2,1:T(8,128)(2,1)} %bitcast.83, pred[1024,1024]{0,1:T(8,128)(4,1)} %broadcast_compare_fusion), kind=kOutput, calls=%fused_computation.97 | convolution fusion | flops 824174592 | bytes 27811840 | tf_op jit(solution)/shard_map/qhe,khe->hqk/dot_general | solution.py:207
  42.6 10.3 %fusion.7 = f32[6,1024]{1,0:T(8,128)S(1)} fusion(f32[6,1024,1024]{1,2,0:T(8,128)} %get-tuple-element.126, f32[6,1024]{1,0:T(8,128)S(1)} %get-tuple-element.125), kind=kLoop, calls=%fused_computation.15 | loop fusion | flops 12576768 | bytes 25214976 | tf_op jit(solution)/shard_map/reduce_sum | solution.py:261
  52.9 10.6 %fusion.31 = bf16[6,64,1024]{2,1,0:T(8,128)(2,1)S(1)} fusion(bf16[1024,6,64]{0,2,1:T(8,128)(2,1)S(1)} %bitcast.98, f32[6,1024,1024]{1,2,0:T(8,128)} %get-tuple-element.126, f32[6,1024]{1,0:T(8,128)S(1)} %fusion.7, f32[6,1024]{1,0:T(8,128)S(1)} %get-tuple-element.125), kind=kOutput, calls=%fused_computation.69 | convolution fusion | flops 824573952 | bytes 26787840 | tf_op jit(solution)/shard_map/hqk,khe->qhe/dot_general | solution.py:264
  67.4 13.8 %while.11 = (s32[]{:T(128)}, f32[18000]{0:T(1024)S(1)}, s32[8,128]{1,0:T(8,128)S(1)}, s32[]{:T(128)}, s32[]{:T(128)}) while((s32[]{:T(128)}, f32[18000]{0:T(1024)S(1)}, s32[8,128]{1,0:T(8,128)S(1)}, s32[]{:T(128)}, s32[]{:T(128)}) %tuple.45), condition=%wide.region_35.36_spmd.clone, body=%wide.region_34.35_spmd.clone.sunk | while | flops 6948003 | bytes 289611 | solution.py:202
  81.9 11.2 %all-reduce.7.cloned.1.call-done = f32[1024,768]{1,0:T(8,128)} async-done(((f32[1024,768]{1,0:T(8,128)}), f32[1024,768]{1,0:T(8,128)}) %all-reduce.7.cloned.1.call-update) | async-done | bytes 3145744 | tf_op jit(solution)/shard_map/psum | solution.py:267
  101.6 8.1 %convert_reduce_fusion = (f32[1536]{0:T(1024)}, bf16[1024,1536]{1,0:T(8,128)(2,1)S(1)}, bf16[1024,1536]{1,0:T(8,128)(2,1)}) fusion(f32[1024,1536]{1,0:T(8,128)S(1)} %fusion.42, f32[1536]{0:T(1024)S(1)} %copy-done.50, bf16[1024,768]{1,0:T(8,128)(2,1)S(1)} %copy-done.14, bf16[1536,768]{1,0:T(8,128)(2,1)S(1)} %copy-done), kind=kOutput, calls=%fused_computation.21 | convolution fusion | flops 2444229120 | bytes 16527360 | tf_op jit(solution)/shard_map/dot_general | solution.py:186
  115.8 88.7 %all-reduce.11.cloned.1.call-done = f32[18000]{0:T(1024)} async-done(((f32[18000]{0:T(1024)}), f32[18000]{0:T(1024)}) %all-reduce.11.cloned.1.call-update) | async-done | bytes 72016 | tf_op jit(solution)/shard_map/psum | solution.py:344
  206.0 8.3 %fusion.41 = f32[768,1536]{1,0:T(8,128)} fusion(bf16[1024,1536]{1,0:T(8,128)(2,1)} %copy-done.55, f32[1024,768]{1,0:T(8,128)} %copy-done.3, f32[768]{0:T(1024)S(1)} %copy-done.51, f32[768]{0:T(1024)S(1)} %copy-done.40, f32[1024]{0:T(1024)S(1)} %fusion.33, f32[1024]{0:T(1024)S(1)} %broadcast_multiply_fusion), kind=kOutput, calls=%fused_computation.92 | convolution fusion | flops 2419851264 | bytes 11024384 | tf_op jit(solution)/shard_map/dot_general | solution.py:180
  214.3 7.4 %reshape.235 = f32[3,256,6,256]{3,2,1,0:T(8,128)} reshape(f32[768,1536]{1,0:T(8,128)} %fusion.41) | data formatting | bytes 9437184 | tf_op jit(solution)/shard_map/reshape | solution.py:145
  221.8 6.8 copy.82
  232.9 6.9 reshape.234
  239.8 6.1 copy.66
  245.9 6.1 fusion.50
  261.8 15.8 %multiply_reduce_fusion = (f32[6,1024]{1,0:T(8,128)S(1)}, f32[6,1024,1024]{1,2,0:T(8,128)}) fusion(f32[6,1024,1024]{1,2,0:T(8,128)} %get-tuple-element.126, f32[6,1024]{1,0:T(8,128)S(1)} %log_add_fusion, bf16[1024,6,64]{0,2,1:T(8,128)(2,1)S(1)} %bitcast.96, bf16[1024,6,64]{0,2,1:T(8,128)(2,1)S(1)} %bitcast.99), kind=kOutput, calls=%fused_computation.10 | convolution fusion | flops 824174592 | bytes 51953664 | tf_op jit(solution)/shard_map/qhe,khe->hqk/dot_general | solution.py:299
  277.6 17.1 %multiply_convert_fusion = bf16[6,1024,1024]{1,2,0:T(8,128)(2,1)S(1)} fusion(f32[6,1024,1024]{1,2,0:T(8,128)} %get-tuple-element.128, f32[6,1024,1024]{1,2,0:T(8,128)} %get-tuple-element.126, f32[6,1024]{1,0:T(8,128)S(1)} %get-tuple-element.127, f32[6,1024]{1,0:T(8,128)S(1)} %log_add_fusion), kind=kLoop, calls=%fused_computation.9 | loop fusion | flops 25165824 | bytes 62963712 | tf_op jit(solution)/shard_map/convert_element_type | solution.py:305
  301.7 9.7 %multiply_convert_fusion.2 = bf16[6,64,1024]{2,1,0:T(8,128)(2,1)} fusion(bf16[1024,6,64]{0,2,1:T(8,128)(2,1)S(1)} %bitcast.82, bf16[6,1024,1024]{1,2,0:T(8,128)(2,1)} %copy-done.2), kind=kOutput, calls=%fused_computation.65 | convolution fusion | flops 806092800 | bytes 14155776 | tf_op jit(solution)/shard_map/hqk,qhe->khe/dot_general | solution.py:309
  311.4 10.3 %fusion.28 = bf16[6,64,1024]{2,1,0:T(8,128)(2,1)S(1)} fusion(bf16[1024,6,64]{0,2,1:T(8,128)(2,1)S(1)} %bitcast.97, f32[6,1024,1024]{1,2,0:T(8,128)} %get-tuple-element.126, f32[6,1024]{1,0:T(8,128)S(1)} %log_add_fusion), kind=kOutput, calls=%fused_computation.68 | convolution fusion | flops 818282496 | bytes 26763264 | tf_op jit(solution)/shard_map/hqk,qhe->khe/dot_general | solution.py:296
  343.8 6.5 reshape.237
  350.3 10.9 %pad_maximum_fusion.x = f32[18,3,256,256]{3,2,1,0:T(8,128)} fusion(f32[6,3,256,256]{3,2,1,0:T(8,128)} %reshape.237, f32[6,3,256,256]{3,2,1,0:T(8,128)} %bitcast.75, f32[6,3,256,256]{3,2,1,0:T(8,128)} %bitcast.76), kind=kLoop, calls=%fused_computation.17 | loop fusion | flops 7077888 | bytes 28311552 | tf_op jit(solution)/shard_map/concatenate | solution.py:142
  361.2 210.7 %shard_map.271 = f32[18,3,256,256]{3,2,1,0:T(8,128)} custom-call(f32[18,3,256,256]{3,2,1,0:T(8,128)} %pad_maximum_fusion.x), custom_call_target="tpu_custom_call" | custom-call | tf_op jit(solution)/shard_map/pallas_call | solution.py:130
  571.8 10.7 %slice_bitcast_fusion = (f32[6,256,3,256]{3,1,2,0:T(8,128)}, f32[3,256,6,256]{3,1,0,2:T(8,128)}, f32[6,3,256,256]{3,2,1,0:T(8,128)}) fusion(f32[18,3,256,256]{3,2,1,0:T(8,128)} %shard_map.271), kind=kLoop, calls=%fused_computation.36 | loop fusion | bytes 28311552 | tf_op jit(solution)/shard_map/transpose | solution.py:154
  582.6 8.0 %slice.49 = f32[1024,3,384]{2,1,0:T(4,128)} reshape(f32[6,3,256,256]{3,2,1,0:T(8,128)} %get-tuple-element.119) | data formatting | bytes 9437184 | tf_op jit(solution)/shard_map/slice | solution.py:157
  590.6 6.5 slice.53
  628.9 74.4 %all-reduce = (f32[768]{0:T(1024)}, f32[768]{0:T(1024)}, f32[2,384]{1,0:T(2,128)}, f32[768]{0:T(1024)}, f32[768]{0:T(1024)}, /*index=5*/f32[768]{0:T(1024)}, f32[1536]{0:T(1024)}, f32[768]{0:T(1024)}) all-reduce(f32[768]{0:T(1024)S(1)} %get-tuple-element.84, ...), channel_id=1, replica_groups=mesh['dp'=16,'tensor'=2] {'dp'}, use_global_device_ids=true, to_apply=%region_18.19 | all-reduce | flops 6912 | bytes 55296 | tf_op jit(solution)/shard_map/psum | solution.py:344
  (217 shorter events, 131.9 us)
Async XLA Ops:
  7.2 94.4 %copy-start = (bf16[1536,768]{1,0:T(8,128)(2,1)S(1)}, bf16[1536,768]{1,0:T(8,128)(2,1)}, u32[]{:S(2)}) copy-start(bf16[1536,768]{1,0:T(8,128)(2,1)} %param.31) | copy-start | bytes 7077892
  7.2 8.4 %copy-start.48 = (f32[2,384]{1,0:T(2,128)S(1)}, f32[2,384]{1,0:T(2,128)}, u32[]{:S(2)}) copy-start(f32[2,384]{1,0:T(2,128)} %param.24) | copy-start | bytes 9220
  7.2 8.4 %copy-start.34 = (f32[768]{0:T(1024)S(1)}, f32[768]{0:T(1024)}, u32[]{:S(2)}) copy-start(f32[768]{0:T(1024)} %param.21) | copy-start | bytes 9220
  7.2 8.4 %copy-start.52 = (f32[768]{0:T(1024)S(1)}, f32[768]{0:T(1024)}, u32[]{:S(2)}) copy-start(f32[768]{0:T(1024)} %param.22) | copy-start | bytes 9220
  7.2 85.9 %all-reduce.7.cloned.1.call-start = ((), (), s32[]{:S(2)}) async-start(), calls=%async_computation | async-start | bytes 6291456 | tf_op jit(solution)/shard_map/psum | solution.py:267
  9.1 11.0 %copy-start.32 = (f32[1024]{0:T(1024)}, f32[1024]{0:T(1024)S(1)}, u32[]{:S(2)}) copy-start(f32[1024]{0:T(1024)S(1)} %broadcast_multiply_fusion.1) | copy-start | bytes 12292
  11.7 8.3 %copy-start.36 = (f32[1024]{0:T(1024)}, f32[1024]{0:T(1024)S(1)}, u32[]{:S(2)}) copy-start(f32[1024]{0:T(1024)S(1)} %fusion.32) | copy-start | bytes 12292
  23.9 18.7 %copy-start.11 = (bf16[1024,384]{0,1:T(8,128)(2,1)}, bf16[1024,384]{0,1:T(8,128)(2,1)S(1)}, u32[]{:S(2)}) copy-start(bf16[1024,384]{0,1:T(8,128)(2,1)S(1)} %copy.59) | copy-start | bytes 2359300
  42.6 10.3 %copy-start.25 = (bf16[1024,384]{0,1:T(8,128)(2,1)S(1)}, bf16[1024,384]{0,1:T(8,128)(2,1)}, u32[]{:S(2)}) copy-start(bf16[1024,384]{0,1:T(8,128)(2,1)} %copy.58) | copy-start | bytes 2359300
  52.9 11.5 %copy-start.30 = (bf16[384,768]{1,0:T(8,128)(2,1)S(1)}, bf16[384,768]{1,0:T(8,128)(2,1)}, u32[]{:S(2)}) copy-start(bf16[384,768]{1,0:T(8,128)(2,1)} %param.25) | copy-start | bytes 1769476
  67.0 137.4 %all-reduce.11.cloned.1.call-start = ((), (), s32[]{:S(2)}) async-start(), calls=%async_computation.2 | async-start | bytes 147456 | tf_op jit(solution)/shard_map/psum | solution.py:344
  67.3 25.8 %copy-start.46 = (f32[768]{0:T(1024)S(1)}, f32[768]{0:T(1024)}, u32[]{:S(2)}) copy-start(f32[768]{0:T(1024)} %param.26) | copy-start | bytes 9220
  81.8 170.2 %all-reduce.9.cloned.1.call-start = ((), (), s32[]{:S(2)}) async-start(), calls=%async_computation.1 | async-start | bytes 6291456 | tf_op jit(solution)/shard_map/psum | solution.py:282
  115.7 502.8 %all-reduce.13.cloned.1.call-start = ((), (), s32[]{:S(2)}) async-start(), calls=%async_computation.3 | async-start | bytes 12582912 | tf_op jit(solution)/shard_map/psum | solution.py:274
  221.8 6.8 copy-start.15
  221.8 6.8 copy-start.56
  261.8 15.9 %copy-start.23 = (bf16[1024,384]{0,1:T(8,128)(2,1)}, bf16[1024,384]{0,1:T(8,128)(2,1)S(1)}, u32[]{:S(2)}) copy-start(bf16[1024,384]{0,1:T(8,128)(2,1)S(1)} %convolution_convert_fusion) | copy-start | bytes 2359300
  277.6 21.7 %copy-start.13 = (bf16[1024,384]{0,1:T(8,128)(2,1)S(1)}, bf16[1024,384]{0,1:T(8,128)(2,1)}, u32[]{:S(2)}) copy-start(bf16[1024,384]{0,1:T(8,128)(2,1)} %copy.60) | copy-start | bytes 2359300
  301.6 28.2 %copy-start.19 = (bf16[6,64,1024]{2,1,0:T(8,128)(2,1)}, bf16[6,64,1024]{2,1,0:T(8,128)(2,1)S(1)}, u32[]{:S(2)}) copy-start(bf16[6,64,1024]{2,1,0:T(8,128)(2,1)S(1)} %multiply_convert_fusion.3) | copy-start | bytes 2359300
  301.7 9.7 %copy-start.24 = (bf16[1024,384]{0,1:T(8,128)(2,1)S(1)}, bf16[1024,384]{0,1:T(8,128)(2,1)}, u32[]{:S(2)}) copy-start(bf16[1024,384]{0,1:T(8,128)(2,1)} %copy-done.23) | copy-start | bytes 2359300
  590.6 10.8 %slice-start.3 = ((s8[4718592]{0:T(1024)(128)(4,1)}), s8[524288]{0:T(1024)(128)(4,1)S(1)}, s32[]{:S(2)}) async-start(s8[4718592]{0:T(1024)(128)(4,1)} %bitcast.79), calls=%async_computation.7 | async-start | bytes 1048576
  612.0 5.8 copy-start.20
  612.0 5.7 copy-start.22
  626.5 76.9 %copy-start.1 = (bf16[1536,768]{1,0:T(8,128)(2,1)S(1)}, bf16[1536,768]{1,0:T(8,128)(2,1)}, u32[]{:S(2)}) copy-start(bf16[1536,768]{1,0:T(8,128)(2,1)} %param.31) | copy-start | bytes 7077892
  (42 other events, 118.4 us)
Sparse Core Ops, SparseCore 0:
  67.2 25.9 all-reduce.6
  100.1 104.3 all-reduce.10
  207.5 23.1 all-reduce.8
  339.9 32.0 all-reduce.12

commit v2 on v0

v2 whole, which is shorter than its diff:
```python
import functools

import jax
import jax.numpy as jnp
from jax import lax
from jax.experimental import pallas as pl
from jax.experimental.pallas import tpu as pltpu
from jax.sharding import PartitionSpec as P

HEAD = 64
VOCAB = 36000
MESH = pl.DeviceIdType.MESH
F32, BF16 = jnp.float32, jnp.bfloat16
BLK = 256
PARTS = 3
SLOTS = 6
LANES = 128


def mm(left, right):
    return jnp.dot(left, right, preferred_element_type=F32)


def mm_t(left, right):
    return lax.dot_general(left, right, (((1,), (1,)), ((), ())), preferred_element_type=F32)


def bit_of(index, mask):
    return lax.rem(lax.div(index, mask), 2)


def rows_at(index, size):
    return pl.ds(pl.multiple_of(index * size, size), size)


class Exchange:
    def __init__(self, n_dp, chunks, parts, slots, g, r, o, ssem, rsem, osem):
        self.chunks, self.parts, self.slots = chunks, parts, slots
        self.g, self.r, self.o = g, r, o
        self.ssem, self.rsem, self.osem = ssem, rsem, osem
        self.rows = g.shape[2]
        self.bits, self.half, self.stages = stage_counts(n_dp)
        self.dp, self.core = lax.axis_index("dp"), lax.axis_index("tensor")

    def mask(self, c, p, k):
        if k >= 3 or self.bits < 3 or p == 0:
            return 1 << k
        if p == 1:
            return 1 << (1, 0, 2)[k]
        if k == 0:
            return 4
        odd = lax.rem(c, 2)
        return 1 + odd if k == 1 else 2 - odd

    def first(self, c, p, depth):
        at = 0
        for k in range(depth):
            at = at + bit_of(self.dp, self.mask(c, p, k)) * (self.rows >> (k + 1))
        return at

    def slot(self, s):
        if s < self.half:
            return pl.ds(self.rows - (self.rows >> s), self.rows >> (s + 1))
        size = self.rows >> self.half
        return pl.ds(self.rows - size + (s - self.half) * size, size)

    def own(self, c, p, depth):
        return pl.ds(pl.multiple_of(self.first(c, p, depth), 8), self.rows >> depth)

    def copy(self, c, p, s):
        flat_end = self.stages - self.half
        k = s if s < flat_end else self.stages - 1 - s
        mask = self.mask(c, p, k)
        bit = bit_of(self.dp, mask)
        if s < self.half:
            size = self.rows >> (s + 1)
            away = pl.ds(pl.multiple_of(self.first(c, p, s) + (1 - bit) * size, 8), size)
            src = self.g.at[c, p, away]
        elif s < flat_end:
            src = self.g.at[c, p, self.own(c, p, self.half)]
        if s < flat_end:
            dst = self.r.at[lax.rem(c, self.slots), p, self.slot(s)]
        else:
            mine = self.own(c, p, k + 1)
            dst = self.o.at[c, p, mine]
            src = self.g.at[c, p, mine] if s == flat_end else dst
        return pltpu.make_async_remote_copy(
            src,
            dst,
            self.ssem.at[c, p, s],
            self.rsem.at[c, p, s],
            device_id=(self.dp + mask * (1 - 2 * bit), self.core),
            device_id_type=MESH,
        )

    def keep(self, c, p):
        mine = self.own(c, p, self.half)
        return pltpu.make_async_copy(self.g.at[c, p, mine], self.o.at[c, p, mine], self.osem.at[c, p])

    def tick(self, tau):
        flat_end = self.stages - self.half
        for s in range(self.stages + 1):
            c = tau - s

            @pl.when((c >= 0) & (c < self.chunks))
            def _():
                for p in range(self.parts):
                    if s > 0:
                        self.copy(c, p, s - 1).wait()
                    if 0 < s <= flat_end:
                        mine = self.own(c, p, min(s, self.half))
                        got = self.r[lax.rem(c, self.slots), p, self.slot(s - 1)]
                        self.g[c, p, mine] = self.g[c, p, mine] + got
                    if s == flat_end:
                        self.keep(c, p).start()
                    if s == flat_end + 1:
                        self.keep(c, p).wait()
                    if s < self.stages:
                        self.copy(c, p, s).start()


def stage_counts(n_dp):
    bits = n_dp.bit_length() - 1
    half = min(bits, 4)
    return bits, half, bits + half


def slot_rows(n_dp, rows):
    bits, half, _ = stage_counts(n_dp)
    return rows - (rows >> half) + (bits - half) * (rows >> half)


def normalise(x):
    c = x - jnp.mean(x, axis=-1, keepdims=True)
    scale = lax.rsqrt(jnp.mean(c * c, axis=-1, keepdims=True) + 1e-05)
    return c * scale, scale


def norm_back(x_hat, scale, grad):
    middle = jnp.mean(grad, axis=-1, keepdims=True)
    along = jnp.mean(grad * x_hat, axis=-1, keepdims=True)
    return (grad - middle - x_hat * along) * scale


def total(x):
    return jnp.sum(x.astype(F32), axis=0, keepdims=True)


def put_rows(ref, row, vector):
    for i in range(vector.shape[1] // LANES):
        ref[0, 0, row + i : row + i + 1, :] = vector[:, i * LANES : (i + 1) * LANES]


def add_rows(ref, row, vector):
    for i in range(vector.shape[1] // LANES):
        at = slice(row + i, row + i + 1)
        ref[0, 0, at, :] = ref[0, 0, at, :] + vector[:, i * LANES : (i + 1) * LANES]


def small_plan(features, head_cols, units, vocab_local):
    plan, at = {}, 0
    for name, size in (
        ("genes", vocab_local),
        ("gain1", features),
        ("shift1", features),
        ("qbias", head_cols),
        ("vbias", head_cols),
        ("obias", features),
        ("gain2", features),
        ("shift2", features),
        ("ubias", units),
        ("dbias", features),
    ):
        count = -(-size // LANES)
        if name == "genes":
            count = -(-count // 8) * 8
        plan[name] = (at, count, size)
        at += count
    return plan, -(-at // 128) * 128


def leftover(j):
    block = 9 + j // 2
    return 13 + block // 3, block % 3, j % 2


def layer(
    n_dp,
    plan,
    lengths,
    genes,
    tok_h,
    cot_h,
    gain1,
    shift1,
    qkvw_h,
    qvb,
    outw_h,
    obias,
    gain2,
    shift2,
    upw_h,
    ubias,
    dnw_h,
    dbias,
    out_h,
    ing_h,
    o,
    o_small,
    tok,
    cot,
    qkvw,
    outw,
    upw,
    dnw,
    norm,
    norm_t,
    qs,
    ks,
    vs,
    x_t,
    ctx,
    dctx,
    dq_t,
    t1,
    t2,
    t3,
    v,
    g,
    r,
    act,
    act_t,
    gu,
    slope,
    dk_sum,
    dv_sum,
    seg,
    sg,
    sr,
    lsem,
    esend,
    erecv,
    ssem,
    rsem,
    osem,
    sssem,
    srsem,
    sosem,
    vfree,
):
    tokens, features = tok.shape
    head_cols = qs.shape[1]
    units = dnw.shape[0]
    rbs = tokens // BLK
    dp, core = lax.axis_index("dp"), lax.axis_index("tensor")
    other = (dp, 1 - core)

    loads = [
        pltpu.make_async_copy(src, dst, lsem.at[i])
        for i, (src, dst) in enumerate(
            ((tok_h, tok), (qkvw_h, qkvw), (outw_h, outw), (upw_h, upw), (cot_h, cot), (dnw_h, dnw))
        )
    ]
    for load in loads:
        load.start()

    bar = pltpu.get_barrier_semaphore()
    bits = n_dp.bit_length() - 1
    for k in range(bits):
        bit = bit_of(dp, 1 << k)
        to = (dp + (1 << k) * (1 - 2 * bit), core)
        pl.semaphore_signal(bar, inc=1, device_id=to, device_id_type=MESH)
    pl.semaphore_signal(bar, inc=1, device_id=other, device_id_type=MESH)

    big = Exchange(n_dp, g.shape[0], PARTS, SLOTS, g, r, o, ssem, rsem, osem)
    small = Exchange(n_dp, 1, 1, 1, sg, sr, o_small, sssem, srsem, sosem)

    def swap(e, src, rb):
        at = rows_at(rb, BLK)
        return pltpu.make_async_remote_copy(
            src.at[at], v.at[at], esend.at[e, rb], erecv.at[e, rb], device_id=other, device_id_type=MESH
        )

    def freed():
        pl.semaphore_signal(vfree, inc=1, device_id=other, device_id_type=MESH)

    def each(body, count=rbs):
        def step(i, carry):
            body(i)
            return carry

        lax.fori_loop(0, count, step, 0)

    def segment(position):
        ends, seg_now = 0, jnp.zeros(position.shape, jnp.int32)
        for i in range(lengths.shape[1]):
            ends = ends + lengths[0, i]
            seg_now = seg_now + (position >= ends).astype(jnp.int32)
        return seg_now

    seg[...] = segment(lax.broadcasted_iota(jnp.int32, (tokens, LANES), 0))
    sg[...] = jnp.zeros_like(sg)

    loads[0].wait()

    def first_norm(rb):
        at = rows_at(rb, BLK)
        x_hat, _ = normalise(tok[at, :].astype(F32))
        norm[at, :] = (x_hat * gain1[...] + shift1[...]).astype(BF16)

    each(first_norm)
    loads[1].wait()

    def project(rb):
        at = rows_at(rb, BLK)
        x = norm[at, :]
        qs[at, :] = (mm(x, qkvw[0]) + qvb[0:1, :]).astype(BF16) * BF16(HEAD**-0.5)
        ks[at, :] = mm(x, qkvw[1]).astype(BF16)
        vs[at, :] = (mm(x, qkvw[2]) + qvb[1:2, :]).astype(BF16)

    each(project)
    loads[2].wait()
    pl.semaphore_wait(bar, bits + 1)

    def attend(rb):
        at = rows_at(rb, BLK)
        seg_row = segment(lax.broadcasted_iota(jnp.int32, (1, tokens), 1))
        same = jnp.concatenate([seg[at, :]] * (tokens // LANES), axis=1) == seg_row
        for pair in range(head_cols // LANES):
            sides = []
            for side in range(2):
                cols = slice(pair * LANES + side * HEAD, pair * LANES + (side + 1) * HEAD)
                scores = jnp.where(same, mm_t(qs[at, cols], ks[:, cols]), -1000000000.0)
                e = jnp.exp(scores - jnp.max(scores, axis=-1, keepdims=True))
                inverse = 1.0 / jnp.sum(e, axis=-1, keepdims=True)
                sides.append(mm((e * inverse).astype(BF16), vs[:, cols]))
            ctx[at, pair * LANES : (pair + 1) * LANES] = jnp.concatenate(sides, axis=1).astype(BF16)
        t1[at, :] = mm(ctx[at, :], outw[...])
        swap(0, t1, rb).start()

    each(attend)
    loads[3].wait()
    loads[4].wait()
    loads[5].wait()

    def second_norm(rb):
        at = rows_at(rb, BLK)
        swap(0, t1, rb).wait()
        hidden = tok[at, :].astype(F32) + (t1[at, :] + v[at, :]) + obias[...]
        t1[at, :] = hidden
        x_hat, _ = normalise(hidden)
        norm[at, :] = (x_hat * gain2[...] + shift2[...]).astype(BF16)
        t2[at, :] = jnp.zeros((BLK, features), F32)
        t3[at, :] = jnp.zeros((BLK, features), F32)

    each(second_norm)
    freed()

    def feed_forward(u):
        ucols = rows_at(u, BLK)

        def upper(rb):
            at = rows_at(rb, BLK)
            up = mm(norm[at, :], upw[:, ucols]) + ubias[:, ucols]
            cdf = 0.5 * (1.0 + lax.erf(up * 0.7071067811865476))
            act[at, :] = (up * cdf).astype(BF16)
            slope[at, :] = cdf + up * (jnp.exp(-0.5 * up * up) * 0.3989422804014327)

        each(upper)
        act_t[...] = act[...].T
        for p in range(PARTS):
            g[2 * u, p] = mm(act_t[...], cot[:, p * BLK : (p + 1) * BLK])
        big.tick(u + jnp.minimum(u, 1))

        @pl.when(u == 0)
        def _():
            norm_t[...] = norm[...].T

        def lower(rb, sums):
            at = rows_at(rb, BLK)
            down_rows = dnw[ucols, :]
            grad = (mm_t(cot[at, :], down_rows) * slope[at, :]).astype(BF16)
            gu[at, :] = grad
            t2[at, :] = t2[at, :] + mm(act[at, :], down_rows)
            t3[at, :] = t3[at, :] + mm_t(grad, upw[:, ucols])
            return sums + total(grad)

        sums = lax.fori_loop(0, rbs, lower, jnp.zeros((1, BLK), F32))
        row = plan["ubias"][0] + u * (BLK // LANES)
        for i in range(BLK // LANES):
            sg[0, 0, pl.ds(row + i, 1), :] = sums[:, i * LANES : (i + 1) * LANES]
        for p in range(PARTS):
            g[2 * u + 1, p] = mm(norm_t[p * BLK : (p + 1) * BLK, :], gu[...])

        @pl.when(u == 0)
        def _():
            big.tick(1)

    each(feed_forward, units // BLK)
    tau = units // BLK + 1

    pl.semaphore_wait(vfree, 1)
    each(lambda rb: swap(1, t3, rb).start())
    big.tick(tau)
    tau += 1

    def second_norm_back(rb):
        at = rows_at(rb, BLK)
        swap(1, t3, rb).wait()
        grad = t3[at, :] + v[at, :]
        x_hat, scale = normalise(t1[at, :])
        add_rows(sg, plan["gain2"][0], total(grad * x_hat))
        add_rows(sg, plan["shift2"][0], total(grad))
        given = cot[at, :].astype(F32)
        add_rows(sg, plan["dbias"][0], total(given))
        grad = given + norm_back(x_hat, scale, grad * gain2[...])
        t3[at, :] = grad
        norm[at, :] = grad.astype(BF16)
        add_rows(sg, plan["obias"][0], total(norm[at, :]))
        dctx[at, :] = mm_t(norm[at, :], outw[...]).astype(BF16)

    each(second_norm_back)
    freed()
    pl.semaphore_wait(vfree, 1)
    each(lambda rb: swap(2, t2, rb).start())

    x_t[...] = ctx[...].T
    for p in range(PARTS):
        branch = norm[:, p * BLK : (p + 1) * BLK]
        g[12, p] = mm(x_t[:BLK, :], branch)
        rest = mm(x_t[BLK:, :], branch)
        if p < 2:
            g[17, 1, p * LANES : (p + 1) * LANES] = rest
        else:
            g[17, 2, :LANES] = rest
    big.tick(tau)
    tau += 1

    def result(rb):
        at = rows_at(rb, BLK)
        swap(2, t2, rb).wait()
        norm[at, :] = (t1[at, :] + (t2[at, :] + v[at, :]) + dbias[...]).astype(BF16)

    each(result)
    freed()
    to_out = pltpu.make_async_copy(norm, out_h, lsem.at[0])
    to_out.start()

    x_t[...] = ks[...].T

    def attend_back(step):
        pair, qb = lax.div(step, rbs), lax.rem(step, rbs)
        at = rows_at(qb, BLK)
        cols = rows_at(pair, LANES)
        position = lax.broadcasted_iota(jnp.int32, (1, BLK), 1) + qb * BLK
        seg_row = segment(position)
        same = jnp.concatenate([seg[...]] * (BLK // LANES), axis=1) == seg_row
        dks, dvs = [], []
        for side in range(2):
            lanes = slice(side * HEAD, (side + 1) * HEAD)
            q_now, d_now = qs[at, cols][:, lanes], dctx[at, cols][:, lanes]
            scores = jnp.where(same, mm_t(ks[:, cols][:, lanes], q_now), -1000000000.0)
            e = jnp.exp(scores - jnp.max(scores, axis=0, keepdims=True))
            probs = e * (1.0 / jnp.sum(e, axis=0, keepdims=True))
            grad = mm_t(vs[:, cols][:, lanes], d_now)
            inner = jnp.sum(probs * grad, axis=0, keepdims=True)
            grad = (probs * (grad - inner)).astype(BF16)
            dvs.append(mm(probs.astype(BF16), d_now))
            dks.append(mm(grad, q_now))
            hrows = pl.ds(pl.multiple_of(pair * LANES + side * HEAD, HEAD), HEAD)
            dq_t[hrows, at] = (mm(x_t[hrows, :], grad) * HEAD**-0.5).astype(BF16)
        dk_now, dv_now = jnp.concatenate(dks, axis=1), jnp.concatenate(dvs, axis=1)

        @pl.when(qb == 0)
        def _():
            dk_sum[...] = dk_now
            dv_sum[...] = dv_now

        @pl.when(qb > 0)
        def _():
            dk_sum[...] = dk_sum[...] + dk_now
            dv_sum[...] = dv_sum[...] + dv_now

        @pl.when(qb == rbs - 1)
        def _():
            ks[:, cols] = dk_sum[...].astype(BF16)
            vs[:, cols] = dv_sum[...].astype(BF16)

        @pl.when(lax.rem(step, 3) == 1)
        def _():
            big.tick(tau + lax.div(step, 3))

    steps = rbs * (head_cols // LANES)
    each(attend_back, steps)
    tau += steps // 3

    qs[...] = dq_t[...].T
    put_rows(sg, plan["qbias"][0], total(qs[...]))
    put_rows(sg, plan["vbias"][0], total(vs[...]))
    to_out.wait()
    each(first_norm)
    norm_t[...] = norm[...].T
    for i, grads in enumerate((qs, ks, vs)):
        for j in range(PARTS):
            made = mm(norm_t[j * BLK : (j + 1) * BLK, :], grads[...])
            g[13 + i, j] = made[:, :BLK]
            if i * 3 + j < 8:
                c, p, side = leftover(i * 3 + j)
                g[c, p, :, side * LANES : (side + 1) * LANES] = made[:, BLK:]
            else:
                g[17, 2, LANES:, :LANES] = made[:LANES, BLK:]
                g[17, 2, LANES:, LANES:] = made[LANES:, BLK:]
    big.tick(tau)
    tau += 1

    pl.semaphore_wait(vfree, 1)

    def to_norm(rb):
        at = rows_at(rb, BLK)
        t2[at, :] = mm_t(qs[at, :], qkvw[0]) + mm_t(ks[at, :], qkvw[1]) + mm_t(vs[at, :], qkvw[2])
        swap(3, t2, rb).start()

    each(to_norm)

    def first_norm_back(rb):
        at = rows_at(rb, BLK)
        swap(3, t2, rb).wait()
        grad = t2[at, :] + v[at, :]
        x_hat, scale = normalise(tok[at, :].astype(F32))
        add_rows(sg, plan["gain1"][0], total(grad * x_hat))
        add_rows(sg, plan["shift1"][0], total(grad))
        norm[at, :] = (t3[at, :] + norm_back(x_hat, scale, grad * gain1[...])).astype(BF16)

    each(first_norm_back)
    to_ing = pltpu.make_async_copy(norm, ing_h, lsem.at[1])
    to_ing.start()

    rows = plan["genes"][1]
    local = genes[...] - core * plan["genes"][2]
    high = lax.shift_right_arithmetic(local, 7)
    low = local - high * LANES
    high = (lax.broadcasted_iota(jnp.int32, (rows, tokens), 0) == high).astype(F32).astype(BF16)
    low = (lax.broadcasted_iota(jnp.int32, (LANES, tokens), 0) == low).astype(F32).astype(BF16)
    sg[0, 0, :rows, :] = mm_t(high, low)

    def finish(i, carry):
        big.tick(tau + i)
        small.tick(i)
        return carry

    left = g.shape[0] + big.stages - tau
    lax.fori_loop(0, max(left, small.stages + 1), finish, 0)
    to_ing.wait()


def run_layer(n_dp, plan, small_rows, *args):
    (lengths, genes, tok, cot, gain1, shift1, qkvw, qvb, outw, obias, gain2, shift2, upw, ubias, dnw, dbias) = args
    tokens, features = tok.shape
    units, head_cols = dnw.shape[0], outw.shape[0]
    chunks = (features * (2 * units + 4 * head_cols)) // (PARTS * BLK * BLK)
    _, _, stages = stage_counts(n_dp)
    vmem = pl.BlockSpec(memory_space=pltpu.VMEM)
    smem = pl.BlockSpec(memory_space=pltpu.SMEM)
    hbm = pl.BlockSpec(memory_space=pl.ANY)
    dma = pltpu.SemaphoreType.DMA
    wide = (tokens, features)
    return pl.pallas_call(
        functools.partial(layer, n_dp, plan),
        out_shape=(
            jax.ShapeDtypeStruct(wide, BF16),
            jax.ShapeDtypeStruct(wide, BF16),
            jax.ShapeDtypeStruct((chunks, PARTS, BLK, BLK), F32),
            jax.ShapeDtypeStruct((1, 1, small_rows, LANES), F32),
        ),
        in_specs=[smem, vmem, hbm, hbm, vmem, vmem, hbm, vmem, hbm, vmem, vmem, vmem, hbm, vmem, hbm, vmem],
        out_specs=(hbm, hbm, hbm, hbm),
        scratch_shapes=[
            pltpu.VMEM(wide, BF16),
            pltpu.VMEM(wide, BF16),
            pltpu.VMEM(qkvw.shape, BF16),
            pltpu.VMEM(outw.shape, BF16),
            pltpu.VMEM(upw.shape, BF16),
            pltpu.VMEM(dnw.shape, BF16),
            pltpu.VMEM(wide, BF16),
            pltpu.VMEM((features, tokens), BF16),
            pltpu.VMEM((tokens, head_cols), BF16),
            pltpu.VMEM((tokens, head_cols), BF16),
            pltpu.VMEM((tokens, head_cols), BF16),
            pltpu.VMEM((head_cols, tokens), BF16),
            pltpu.VMEM((tokens, head_cols), BF16),
            pltpu.VMEM((tokens, head_cols), BF16),
            pltpu.VMEM((head_cols, tokens), BF16),
            pltpu.VMEM(wide, F32),
            pltpu.VMEM(wide, F32),
            pltpu.VMEM(wide, F32),
            pltpu.VMEM(wide, F32),
            pltpu.VMEM((chunks, PARTS, BLK, BLK), F32),
            pltpu.VMEM((SLOTS, PARTS, slot_rows(n_dp, BLK), BLK), F32),
            pltpu.VMEM((tokens, BLK), BF16),
            pltpu.VMEM((BLK, tokens), BF16),
            pltpu.VMEM((tokens, BLK), BF16),
            pltpu.VMEM((tokens, BLK), F32),
            pltpu.VMEM((tokens, LANES), F32),
            pltpu.VMEM((tokens, LANES), F32),
            pltpu.VMEM((tokens, LANES), jnp.int32),
            pltpu.VMEM((1, 1, small_rows, LANES), F32),
            pltpu.VMEM((1, 1, slot_rows(n_dp, small_rows), LANES), F32),
            dma((6,)),
            dma((4, tokens // BLK)),
            dma((4, tokens // BLK)),
            dma((chunks, PARTS, stages)),
            dma((chunks, PARTS, stages)),
            dma((chunks, PARTS)),
            dma((1, 1, stages)),
            dma((1, 1, stages)),
            dma((1, 1)),
            pltpu.SemaphoreType.REGULAR,
        ],
        compiler_params=pltpu.CompilerParams(
            collective_id=0, has_side_effects=True, vmem_limit_bytes=63 << 20
        ),
    )(*args)


def unpack(packed, features, units, head_cols):
    down = packed[0:12:2].transpose(0, 2, 1, 3).reshape(units, features)
    up = packed[1:12:2].transpose(1, 2, 0, 3).reshape(features, units)
    out = jnp.concatenate(
        [
            packed[12].transpose(1, 0, 2).reshape(BLK, features),
            jnp.concatenate([packed[17, 1, :LANES], packed[17, 1, LANES:], packed[17, 2, :LANES]], axis=1),
        ],
        axis=0,
    )
    pieces = []
    for i in range(3):
        rows = []
        for j in range(3):
            if i * 3 + j < 8:
                c, p, side = leftover(i * 3 + j)
                rest = packed[c, p, :, side * LANES : (side + 1) * LANES]
            else:
                rest = jnp.concatenate([packed[17, 2, LANES:, :LANES], packed[17, 2, LANES:, LANES:]], axis=0)
            rows.append(jnp.concatenate([packed[13 + i, j], rest], axis=1))
        pieces.append(jnp.concatenate(rows, axis=0))
    return down, up, out, jnp.stack(pieces, axis=1)


def on_device(
    n_dp,
    tokens,
    lengths,
    gene_ids,
    norm1_gain,
    norm1_shift,
    qkv_weight,
    qv_bias,
    out_weight,
    out_bias,
    norm2_gain,
    norm2_shift,
    up_weight,
    up_bias,
    down_weight,
    down_bias,
    cotangent,
):
    features = tokens.shape[1]
    head_cols, units = out_weight.shape[0], down_weight.shape[0]
    plan, small_rows = small_plan(features, head_cols, units, VOCAB // lax.axis_size("tensor"))
    output, input_grad, packed, sums = run_layer(
        n_dp,
        plan,
        small_rows,
        lengths,
        gene_ids[None],
        tokens,
        cotangent,
        norm1_gain[None],
        norm1_shift[None],
        qkv_weight.transpose(1, 0, 2),
        qv_bias,
        out_weight,
        out_bias[None],
        norm2_gain[None],
        norm2_shift[None],
        up_weight,
        up_bias[None],
        down_weight,
        down_bias[None],
    )
    down_grad, up_grad, out_grad, qkv_grad = unpack(packed, features, units, head_cols)

    def take(name):
        at, count, size = plan[name]
        return sums[0, 0, at : at + count].reshape(-1)[:size]

    return (
        output,
        input_grad,
        take("gain1"),
        take("shift1"),
        qkv_grad,
        jnp.stack([take("qbias"), take("vbias")]),
        out_grad,
        take("obias"),
        take("gain2"),
        take("shift2"),
        up_grad,
        take("ubias"),
        down_grad,
        take("dbias"),
        take("genes").astype(jnp.int32),
    )


def solution(mesh):
    return jax.shard_map(
        functools.partial(on_device, mesh.shape["dp"]),
        mesh=mesh,
        in_specs=(
            P("dp", None),
            P("dp", None),
            P("dp"),
            P(),
            P(),
            P(None, None, "tensor"),
            P(None, "tensor"),
            P("tensor", None),
            P(),
            P(),
            P(),
            P(None, "tensor"),
            P("tensor"),
            P("tensor", None),
            P(),
            P("dp", None),
        ),
        out_specs=(
            P("dp", None),
            P("dp", None),
            P(),
            P(),
            P(None, None, "tensor"),
            P(None, "tensor"),
            P("tensor", None),
            P(),
            P(),
            P(),
            P(None, "tensor"),
            P("tensor"),
            P("tensor", None),
            P(),
            P("tensor"),
        ),
        check_vma=False,
    )
```

time: 694 us -> 293 us (0.42); the launches traced: 686 us -> 292 us
  waiting for transfers between devices: 352 us -> 0 us
  Pallas kernels: 0 us -> 244 us
  matrix products: 129 us -> 0 us
  blocking collectives: 81.9 us -> 0 us
  other arithmetic: 58.4 us -> 3.6 us
  between operations: 14.5 us -> 0.76 us
  starting transfers between devices: 9.96 us -> 0 us
    psum x4 -> x0, waiting for transfers between devices: 352 us -> none  [the longest x1 318 us: on_device(): lax.psum((norm1_gain_grad, norm1_shift_grad, qkv_grad, qv_bias_grad, out_...]
    pallas_call x0 -> x1, Pallas kernels: none -> 244 us  [run_layer(): pl.pallas_call(functools.partial(layer, n_dp, plan), out_shape=(jax.Shape...]
    dot_general x26 -> x0, matrix products: 129 us -> none  [the longest x4 18.3 us: by_transpose(): lax.dot_general(left, right, (((1,), (1,)), ((), ())), preferred_element_...]
    psum x1 -> x0, blocking collectives: 81.9 us -> none  [on_device(): lax.psum((norm1_gain_grad, norm1_shift_grad, qkv_grad, qv_bias_grad, out_...]
    reduce_sum x13 -> x0, other arithmetic: 30.7 us -> none  [the longest x1 10.3 us: on_device(): row_sum = jnp.sum(exponent, axis=-1, keepdims=True)]
    convert_element_type x5 -> x1, other arithmetic: 25.7 us -> 0.64 us  [on_device(): take('genes').astype(jnp.int32)]
    unnamed x109 -> x11, local copies, waits for them, and re-layouts: 32.8 us -> 16.4 us
    psum x4 -> x0, starting transfers between devices: 9.96 us -> none  [the longest x1 9.84 us: on_device(): grad_normed2 = lax.psum(by_transpose(grad_upper, up_weight), 'tensor')]
  transfers between devices with their start and end apart: 4 -> 0, of which waited for: 3 -> 0; matrix products, arithmetic and copies ran while one was open for 7% -> 0% of each run, Pallas kernels for 0% -> 0%
where the time goes in v2:
time: 293 us; the launch traced here: 292 us
  Pallas kernels  244 us (83%)
  local copies, waits for them, and re-layouts  43.3 us (15%)
  other arithmetic  3.6 us (1%)
    pallas_call x1, Pallas kernels, run_layer(): pl.pallas_call(functools.partial(layer, n_dp, plan), out_shape=(jax.Shape...  244 us
    unnamed x11, local copies, waits for them, and re-layouts  16.4 us

profile of v2, /device:TPU:0, one launch (start us, length us, event | category | flops | bytes accessed | tf_op | source)
XLA Modules:
  0.0 291.9 jit_solution(12166329205249753883)
XLA Ops:
  0.6 1.3 broadcast_in_dim.25.gain1
  1.9 1.3 broadcast_in_dim.26.shift1
  3.2 1.3 broadcast_in_dim.27.obias
  4.4 1.3 broadcast_in_dim.28.gain2
  5.7 1.3 broadcast_in_dim.29.shift2
  7.0 1.3 broadcast_in_dim.31.dbias
  8.2 1.3 broadcast_in_dim.30.ubias
  9.5 244.2 %shard_map.271 = (bf16[1024,768]{1,0:T(8,128)(2,1)}, bf16[1024,768]{1,0:T(8,128)(2,1)}, f32[18,3,256,256]{3,2,1,0:T(8,128)}, f32[1,1,256,128]{3,2,1,0:T(8,128)}) custom-call(s32[1,6]{1,0:T(1,128)} %lengths.1, s32[1,1024]{1,0:T(1,128)} %bitcast.99, bf16[1024,768]{1,0:T(8,128)(2,1)} %tok_h.1, bf16[1024,768]{1,0:T(8,128)(2,1)} %cot_h.1, ...), custom_call_target="tpu_custom_call" | custom-call | tf_op jit(solution)/shard_map/pallas_call | solution.py:567
  255.1 1.3 slice_bitcast_fusion.26
  256.4 1.4 slice_bitcast_fusion.27
  257.8 0.9 slice_bitcast_fusion.23
  260.2 1.1 slice_bitcast_fusion.14
  261.4 1.2 slice_bitcast_fusion.2
  263.0 1.4 copy.35
  264.4 1.4 slice_bitcast_fusion.22
  265.7 1.8 slice_bitcast_fusion.11
  267.6 4.8 %slice_bitcast_fusion = (f32[6,256,3,256]{3,1,2,0:T(8,128)S(1)}, f32[3,256,6,256]{3,1,0,2:T(8,128)S(1)}) fusion(f32[18,3,256,256]{3,2,1,0:T(8,128)} %get-tuple-element.22), kind=kLoop, calls=%fused_computation | loop fusion | bytes 18874368 | tf_op jit(solution)/shard_map/transpose | solution.py:626
  272.7 2.0 pad_maximum_fusion
  274.7 3.2 %copy.37 = f32[6,256,3,256]{3,2,1,0:T(4,128)S(1)} copy(f32[6,256,3,256]{3,1,2,0:T(8,128)S(1)} %get-tuple-element.38) | data formatting | bytes 9437184
  277.9 3.3 %copy.42 = f32[192,8,3,256]{3,1,2,0:T(8,128)} copy(f32[192,8,3,256]{3,2,1,0:T(4,128)S(1)} %bitcast.93) | data formatting | bytes 9437184
  281.3 3.0 %copy.33 = f32[3,256,6,256]{3,2,1,0:T(8,128)S(1)} copy(f32[3,256,6,256]{3,1,0,2:T(8,128)S(1)} %get-tuple-element.39) | data formatting | bytes 9437184 | tf_op jit(solution)/shard_map/transpose | solution.py:627
  284.2 4.5 %copy.41 = f32[96,8,6,256]{3,1,2,0:T(8,128)} copy(f32[96,8,6,256]{3,2,1,0:T(8,128)S(1)} %bitcast.94) | data formatting | bytes 9437184
  288.7 1.1 copy.47
  290.7 1.1 copy.48
  (15 shorter events, 4.5 us)
Async XLA Ops:
  284.2 4.5 %copy-start.1 = (bf16[1024,768]{1,0:T(8,128)(2,1)S(1)}, bf16[1024,768]{1,0:T(8,128)(2,1)}, u32[]{:S(2)}) copy-start(bf16[1024,768]{1,0:T(8,128)(2,1)} %get-tuple-element.89) | copy-start | bytes 4718596
  288.7 2.0 copy-start

commit v3 on v2

--- a/solution.py
+++ b/solution.py
@@ -306,7 +306,7 @@
     def first_norm(rb):
         at = rows_at(rb, BLK)
         x_hat, _ = normalise(tok[at, :].astype(F32))
-        norm[at, :] = (x_hat * gain1[...] + shift1[...]).astype(BF16)
+        norm[at, :] = (x_hat * gain1[...][None, :] + shift1[...][None, :]).astype(BF16)
 
     each(first_norm)
     loads[1].wait()
@@ -346,10 +346,10 @@
     def second_norm(rb):
         at = rows_at(rb, BLK)
         swap(0, t1, rb).wait()
-        hidden = tok[at, :].astype(F32) + (t1[at, :] + v[at, :]) + obias[...]
+        hidden = tok[at, :].astype(F32) + (t1[at, :] + v[at, :]) + obias[...][None, :]
         t1[at, :] = hidden
         x_hat, _ = normalise(hidden)
-        norm[at, :] = (x_hat * gain2[...] + shift2[...]).astype(BF16)
+        norm[at, :] = (x_hat * gain2[...][None, :] + shift2[...][None, :]).astype(BF16)
         t2[at, :] = jnp.zeros((BLK, features), F32)
         t3[at, :] = jnp.zeros((BLK, features), F32)
 
@@ -361,7 +361,7 @@
 
         def upper(rb):
             at = rows_at(rb, BLK)
-            up = mm(norm[at, :], upw[:, ucols]) + ubias[:, ucols]
+            up = mm(norm[at, :], upw[:, ucols]) + ubias[ucols][None, :]
             cdf = 0.5 * (1.0 + lax.erf(up * 0.7071067811865476))
             act[at, :] = (up * cdf).astype(BF16)
             slope[at, :] = cdf + up * (jnp.exp(-0.5 * up * up) * 0.3989422804014327)
@@ -413,7 +413,7 @@
         add_rows(sg, plan["shift2"][0], total(grad))
         given = cot[at, :].astype(F32)
         add_rows(sg, plan["dbias"][0], total(given))
-        grad = given + norm_back(x_hat, scale, grad * gain2[...])
+        grad = given + norm_back(x_hat, scale, grad * gain2[...][None, :])
         t3[at, :] = grad
         norm[at, :] = grad.astype(BF16)
         add_rows(sg, plan["obias"][0], total(norm[at, :]))
@@ -439,7 +439,7 @@
     def result(rb):
         at = rows_at(rb, BLK)
         swap(2, t2, rb).wait()
-        norm[at, :] = (t1[at, :] + (t2[at, :] + v[at, :]) + dbias[...]).astype(BF16)
+        norm[at, :] = (t1[at, :] + (t2[at, :] + v[at, :]) + dbias[...][None, :]).astype(BF16)
 
     each(result)
     freed()
@@ -529,14 +529,14 @@
         x_hat, scale = normalise(tok[at, :].astype(F32))
         add_rows(sg, plan["gain1"][0], total(grad * x_hat))
         add_rows(sg, plan["shift1"][0], total(grad))
-        norm[at, :] = (t3[at, :] + norm_back(x_hat, scale, grad * gain1[...])).astype(BF16)
+        norm[at, :] = (t3[at, :] + norm_back(x_hat, scale, grad * gain1[...][None, :])).astype(BF16)
 
     each(first_norm_back)
     to_ing = pltpu.make_async_copy(norm, ing_h, lsem.at[1])
     to_ing.start()
 
     rows = plan["genes"][1]
-    local = genes[...] - core * plan["genes"][2]
+    local = genes[...][None, :] - core * plan["genes"][2]
     high = lax.shift_right_arithmetic(local, 7)
     low = local - high * LANES
     high = (lax.broadcasted_iota(jnp.int32, (rows, tokens), 0) == high).astype(F32).astype(BF16)
@@ -622,28 +622,109 @@
     )(*args)
 
 
-def unpack(packed, features, units, head_cols):
-    down = packed[0:12:2].transpose(0, 2, 1, 3).reshape(units, features)
-    up = packed[1:12:2].transpose(1, 2, 0, 3).reshape(features, units)
-    out = jnp.concatenate(
-        [
-            packed[12].transpose(1, 0, 2).reshape(BLK, features),
-            jnp.concatenate([packed[17, 1, :LANES], packed[17, 1, LANES:], packed[17, 2, :LANES]], axis=1),
-        ],
-        axis=0,
-    )
-    pieces = []
+def hand_out(plan, packed_h, sums, out_h, ing_h, *refs):
+    (output, input_grad, gain1, shift1, qkv, qv, out, obias, gain2, shift2, up, ubias, down, dbias, genes) = refs[:15]
+    packed, wide, loaded, sem = refs[15:]
+    chunks = packed.shape[0]
+    loads = [pltpu.make_async_copy(packed_h.at[c], packed.at[c], loaded.at[c]) for c in range(chunks)]
+    loads.append(pltpu.make_async_copy(out_h, wide.at[0], loaded.at[chunks]))
+    loads.append(pltpu.make_async_copy(ing_h, wide.at[1], loaded.at[chunks + 1]))
+    for load in loads:
+        load.start()
+    moves = [[] for load in loads]
+    moves[chunks].append((wide.at[0], output))
+    moves[chunks + 1].append((wide.at[1], input_grad))
+    for u in range(down.shape[0] // BLK):
+        for p in range(PARTS):
+            units, cols = pl.ds(u * BLK, BLK), pl.ds(p * BLK, BLK)
+            moves[2 * u].append((packed.at[2 * u, p], down.at[units, cols]))
+            moves[2 * u + 1].append((packed.at[2 * u + 1, p], up.at[cols, units]))
+    half = pl.ds(0, LANES), pl.ds(LANES, LANES)
+    for p in range(PARTS):
+        cols = pl.ds(p * BLK, BLK)
+        moves[12].append((packed.at[12, p], out.at[pl.ds(0, BLK), cols]))
+        rest = packed.at[17, 1 + p // 2, half[p % 2]]
+        moves[17].append((rest, out.at[pl.ds(BLK, LANES), cols]))
     for i in range(3):
-        rows = []
-        for j in range(3):
+        for j in range(PARTS):
+            rows, tail = pl.ds(j * BLK, BLK), pl.ds(BLK, LANES)
+            moves[13 + i].append((packed.at[13 + i, j], qkv.at[i, rows, pl.ds(0, BLK)]))
             if i * 3 + j < 8:
                 c, p, side = leftover(i * 3 + j)
-                rest = packed[c, p, :, side * LANES : (side + 1) * LANES]
+                moves[c].append((packed.at[c, p, pl.ds(0, BLK), half[side]], qkv.at[i, rows, tail]))
             else:
-                rest = jnp.concatenate([packed[17, 2, LANES:, :LANES], packed[17, 2, LANES:, LANES:]], axis=0)
-            rows.append(jnp.concatenate([packed[13 + i, j], rest], axis=1))
-        pieces.append(jnp.concatenate(rows, axis=0))
-    return down, up, out, jnp.stack(pieces, axis=1)
+                for side in range(2):
+                    rows = pl.ds(j * BLK + side * LANES, LANES)
+                    moves[17].append((packed.at[17, 2, half[1], half[side]], qkv.at[i, rows, tail]))
+    copies = []
+    for load, group in zip(loads, moves):
+        load.wait()
+        for src, dst in group:
+            copy = pltpu.make_async_copy(src, dst, sem.at[len(copies)])
+            copy.start()
+            copies.append(copy)
+
+    def vector(name, ref, *index):
+        at, count, _ = plan[name]
+        for i in range(count):
+            ref[(*index, pl.ds(i * LANES, LANES))] = sums[0, 0, at + i]
+
+    for name, ref in (
+        ("gain1", gain1),
+        ("shift1", shift1),
+        ("obias", obias),
+        ("gain2", gain2),
+        ("shift2", shift2),
+        ("ubias", ubias),
+        ("dbias", dbias),
+    ):
+        vector(name, ref)
+    vector("qbias", qv, 0)
+    vector("vbias", qv, 1)
+    size = plan["genes"][2]
+    for i in range(-(-size // LANES)):
+        part = min(LANES, size - i * LANES)
+        genes[pl.ds(i * LANES, part)] = sums[0, 0, i, :part].astype(jnp.int32)
+    for copy in copies:
+        copy.wait()
+
+
+def results(plan, features, head_cols, units, packed, sums, output, input_grad):
+    vmem = pl.BlockSpec(memory_space=pltpu.VMEM)
+    hbm = pl.BlockSpec(memory_space=pl.ANY)
+    size = lambda name: (plan[name][2],)
+    shapes = (
+        output.shape,
+        input_grad.shape,
+        size("gain1"),
+        size("shift1"),
+        (3, features, head_cols),
+        (2, head_cols),
+        (head_cols, features),
+        size("obias"),
+        size("gain2"),
+        size("shift2"),
+        (features, units),
+        size("ubias"),
+        (units, features),
+        size("dbias"),
+        size("genes"),
+    )
+    types = [BF16, BF16] + [F32] * 12 + [jnp.int32]
+    large = (0, 1, 4, 6, 10, 12)
+    return pl.pallas_call(
+        functools.partial(hand_out, plan),
+        out_shape=tuple(jax.ShapeDtypeStruct(shape, kind) for shape, kind in zip(shapes, types)),
+        in_specs=[hbm, vmem, hbm, hbm],
+        out_specs=tuple(hbm if i in large else vmem for i in range(15)),
+        scratch_shapes=[
+            pltpu.VMEM(packed.shape, F32),
+            pltpu.VMEM((2, *output.shape), BF16),
+            pltpu.SemaphoreType.DMA((packed.shape[0] + 2,)),
+            pltpu.SemaphoreType.DMA((80,)),
+        ],
+        compiler_params=pltpu.CompilerParams(vmem_limit_bytes=60 << 20),
+    )(packed, sums, output, input_grad)
 
 
 def on_device(
@@ -673,45 +754,25 @@
         plan,
         small_rows,
         lengths,
-        gene_ids[None],
+        gene_ids,
         tokens,
         cotangent,
-        norm1_gain[None],
-        norm1_shift[None],
+        norm1_gain,
+        norm1_shift,
         qkv_weight.transpose(1, 0, 2),
         qv_bias,
         out_weight,
-        out_bias[None],
-        norm2_gain[None],
-        norm2_shift[None],
+        out_bias,
+        norm2_gain,
+        norm2_shift,
         up_weight,
-        up_bias[None],
+        up_bias,
         down_weight,
-        down_bias[None],
+        down_bias,
     )
-    down_grad, up_grad, out_grad, qkv_grad = unpack(packed, features, units, head_cols)
-
-    def take(name):
-        at, count, size = plan[name]
-        return sums[0, 0, at : at + count].reshape(-1)[:size]
-
-    return (
-        output,
-        input_grad,
-        take("gain1"),
-        take("shift1"),
-        qkv_grad,
-        jnp.stack([take("qbias"), take("vbias")]),
-        out_grad,
-        take("obias"),
-        take("gain2"),
-        take("shift2"),
-        up_grad,
-        take("ubias"),
-        down_grad,
-        take("dbias"),
-        take("genes").astype(jnp.int32),
-    )
+    made = list(results(plan, features, head_cols, units, packed, sums, output, input_grad))
+    made[4] = made[4].transpose(1, 0, 2)
+    return tuple(made)
 
 
 def solution(mesh):

time: 293 us -> 260 us (0.89)
  local copies, waits for them, and re-layouts: 43.3 us -> 0 us
  Pallas kernels: 244 us -> 259 us
  other arithmetic: 3.6 us -> 0 us
    unnamed x11 -> x0, local copies, waits for them, and re-layouts: 16.4 us -> none
    pallas_call x0 -> x1, Pallas kernels: none -> 14.4 us  [results(): pl.pallas_call(functools.partial(hand_out, plan), out_shape=tuple((jax.Sh...]
    transpose x4 -> x0, local copies, waits for them, and re-layouts: 9.24 us -> none  [the longest x1 4.83 us: unpack(): down = packed[0:12:2].transpose(0, 2, 1, 3).reshape(units, features)]
    broadcast_in_dim x7 -> x0, local copies, waits for them, and re-layouts: 8.89 us -> none  [the longest x1 1.29 us: on_device(): up_bias[None]]
    squeeze x4 -> x0, local copies, waits for them, and re-layouts: 5.12 us -> none  [the longest x1 1.83 us: unpack(): rows.append(jnp.concatenate([packed[13 + i, j], rest], axis=1))]
    another operation x4 -> x0, local copies, waits for them, and re-layouts: 3.57 us -> none  [the longest x3 3.57 us: take(): return sums[0, 0, at:at + count].reshape(-1)[:size]]
where the time goes in v3:
time: 260 us; the launch traced here: 259 us
  Pallas kernels  259 us (100%)
    pallas_call x1, Pallas kernels, run_layer(): pl.pallas_call(functools.partial(layer, n_dp, plan), out_shape=(jax.Shape...  244 us
    pallas_call x1, Pallas kernels, results(): pl.pallas_call(functools.partial(hand_out, plan), out_shape=tuple((jax.Sh...  14.4 us

profile of v3, /device:TPU:0, one launch (start us, length us, event | category | flops | bytes accessed | tf_op | source)
XLA Modules:
  0.0 259.4 jit_solution(14042340062283725429)
XLA Ops:
  0.7 244.1 %shard_map.271 = (bf16[1024,768]{1,0:T(8,128)(2,1)}, bf16[1024,768]{1,0:T(8,128)(2,1)}, f32[18,3,256,256]{3,2,1,0:T(8,128)}, f32[1,1,256,128]{3,2,1,0:T(8,128)}) custom-call(s32[1,6]{1,0:T(1,128)} %lengths.1, s32[1024]{0:T(1024)} %genes.1, bf16[1024,768]{1,0:T(8,128)(2,1)} %tok_h.1, bf16[1024,768]{1,0:T(8,128)(2,1)} %cot_h.1, f32[768]{0:T(1024)} %gain1.1, ...), custom_call_target="tpu_custom_call" | custom-call | tf_op jit(solution)/shard_map/pallas_call | solution.py:567
  244.8 14.4 %shard_map.272 = (bf16[1024,768]{1,0:T(8,128)(2,1)}, bf16[1024,768]{1,0:T(8,128)(2,1)}, f32[768]{0:T(1024)}, f32[768]{0:T(1024)}, f32[3,768,384]{2,1,0:T(8,128)}...) custom-call(f32[18,3,256,256]{3,2,1,0:T(8,128)} %get-tuple-element.3, ...), custom_call_target="tpu_custom_call" | custom-call | tf_op jit(solution)/shard_map/pallas_call | solution.py:715

commit v4 on v3

--- a/solution.py
+++ b/solution.py
@@ -13,7 +13,8 @@
 F32, BF16 = jnp.float32, jnp.bfloat16
 BLK = 256
 PARTS = 3
-SLOTS = 6
+SLOTS = 4
+HELD = 14
 LANES = 128
 
 
@@ -58,6 +59,9 @@
             at = at + bit_of(self.dp, self.mask(c, p, k)) * (self.rows >> (k + 1))
         return at
 
+    def held(self, c):
+        return lax.rem(c, self.g.shape[0])
+
     def slot(self, s):
         if s < self.half:
             return pl.ds(self.rows - (self.rows >> s), self.rows >> (s + 1))
@@ -75,15 +79,15 @@
         if s < self.half:
             size = self.rows >> (s + 1)
             away = pl.ds(pl.multiple_of(self.first(c, p, s) + (1 - bit) * size, 8), size)
-            src = self.g.at[c, p, away]
+            src = self.g.at[self.held(c), p, away]
         elif s < flat_end:
-            src = self.g.at[c, p, self.own(c, p, self.half)]
+            src = self.g.at[self.held(c), p, self.own(c, p, self.half)]
         if s < flat_end:
             dst = self.r.at[lax.rem(c, self.slots), p, self.slot(s)]
         else:
             mine = self.own(c, p, k + 1)
             dst = self.o.at[c, p, mine]
-            src = self.g.at[c, p, mine] if s == flat_end else dst
+            src = self.g.at[self.held(c), p, mine] if s == flat_end else dst
         return pltpu.make_async_remote_copy(
             src,
             dst,
@@ -95,7 +99,7 @@
 
     def keep(self, c, p):
         mine = self.own(c, p, self.half)
-        return pltpu.make_async_copy(self.g.at[c, p, mine], self.o.at[c, p, mine], self.osem.at[c, p])
+        return pltpu.make_async_copy(self.g.at[self.held(c), p, mine], self.o.at[c, p, mine], self.osem.at[c, p])
 
     def tick(self, tau):
         flat_end = self.stages - self.half
@@ -110,7 +114,8 @@
                     if 0 < s <= flat_end:
                         mine = self.own(c, p, min(s, self.half))
                         got = self.r[lax.rem(c, self.slots), p, self.slot(s - 1)]
-                        self.g[c, p, mine] = self.g[c, p, mine] + got
+                        at = self.held(c)
+                        self.g[at, p, mine] = self.g[at, p, mine] + got
                     if s == flat_end:
                         self.keep(c, p).start()
                     if s == flat_end + 1:
@@ -181,7 +186,7 @@
 
 def leftover(j):
     block = 9 + j // 2
-    return 13 + block // 3, block % 3, j % 2
+    return (17, 13)[block // 3 - 3], block % 3, j % 2
 
 
 def layer(
@@ -203,8 +208,8 @@
     ubias,
     dnw_h,
     dbias,
-    out_h,
-    ing_h,
+    out_ref,
+    ing_ref,
     o,
     o_small,
     tok,
@@ -213,15 +218,11 @@
     outw,
     upw,
     dnw,
-    norm,
     norm_t,
     qs,
     ks,
     vs,
-    x_t,
     ctx,
-    dctx,
-    dq_t,
     t1,
     t2,
     t3,
@@ -232,8 +233,6 @@
     act_t,
     gu,
     slope,
-    dk_sum,
-    dv_sum,
     seg,
     sg,
     sr,
@@ -252,6 +251,9 @@
     head_cols = qs.shape[1]
     units = dnw.shape[0]
     rbs = tokens // BLK
+    dq_t, x_t = norm_t.at[:head_cols], norm_t.at[head_cols : 2 * head_cols]
+    dctx, norm = ctx, ing_ref
+    dk_sum, dv_sum = slope.at[:, :LANES], slope.at[:, LANES:]
     dp, core = lax.axis_index("dp"), lax.axis_index("tensor")
     other = (dp, 1 - core)
 
@@ -272,7 +274,7 @@
         pl.semaphore_signal(bar, inc=1, device_id=to, device_id_type=MESH)
     pl.semaphore_signal(bar, inc=1, device_id=other, device_id_type=MESH)
 
-    big = Exchange(n_dp, g.shape[0], PARTS, SLOTS, g, r, o, ssem, rsem, osem)
+    big = Exchange(n_dp, o.shape[0], PARTS, SLOTS, g, r, o, ssem, rsem, osem)
     small = Exchange(n_dp, 1, 1, 1, sg, sr, o_small, sssem, srsem, sosem)
 
     def swap(e, src, rb):
@@ -404,6 +406,8 @@
     big.tick(tau)
     tau += 1
 
+    x_t[...] = ctx[...].T
+
     def second_norm_back(rb):
         at = rows_at(rb, BLK)
         swap(1, t3, rb).wait()
@@ -424,27 +428,24 @@
     pl.semaphore_wait(vfree, 1)
     each(lambda rb: swap(2, t2, rb).start())
 
-    x_t[...] = ctx[...].T
     for p in range(PARTS):
         branch = norm[:, p * BLK : (p + 1) * BLK]
         g[12, p] = mm(x_t[:BLK, :], branch)
         rest = mm(x_t[BLK:, :], branch)
         if p < 2:
-            g[17, 1, p * LANES : (p + 1) * LANES] = rest
+            g[13, 1, p * LANES : (p + 1) * LANES] = rest
         else:
-            g[17, 2, :LANES] = rest
+            g[13, 2, :LANES] = rest
     big.tick(tau)
     tau += 1
 
     def result(rb):
         at = rows_at(rb, BLK)
         swap(2, t2, rb).wait()
-        norm[at, :] = (t1[at, :] + (t2[at, :] + v[at, :]) + dbias[...][None, :]).astype(BF16)
+        out_ref[at, :] = (t1[at, :] + (t2[at, :] + v[at, :]) + dbias[...][None, :]).astype(BF16)
 
     each(result)
     freed()
-    to_out = pltpu.make_async_copy(norm, out_h, lsem.at[0])
-    to_out.start()
 
     x_t[...] = ks[...].T
 
@@ -497,19 +498,18 @@
     qs[...] = dq_t[...].T
     put_rows(sg, plan["qbias"][0], total(qs[...]))
     put_rows(sg, plan["vbias"][0], total(vs[...]))
-    to_out.wait()
     each(first_norm)
     norm_t[...] = norm[...].T
     for i, grads in enumerate((qs, ks, vs)):
         for j in range(PARTS):
             made = mm(norm_t[j * BLK : (j + 1) * BLK, :], grads[...])
-            g[13 + i, j] = made[:, :BLK]
+            g[(14 + i) % HELD, j] = made[:, :BLK]
             if i * 3 + j < 8:
                 c, p, side = leftover(i * 3 + j)
-                g[c, p, :, side * LANES : (side + 1) * LANES] = made[:, BLK:]
+                g[c % HELD, p, :, side * LANES : (side + 1) * LANES] = made[:, BLK:]
             else:
-                g[17, 2, LANES:, :LANES] = made[:LANES, BLK:]
-                g[17, 2, LANES:, LANES:] = made[LANES:, BLK:]
+                g[13, 2, LANES:, :LANES] = made[:LANES, BLK:]
+                g[13, 2, LANES:, LANES:] = made[LANES:, BLK:]
     big.tick(tau)
     tau += 1
 
@@ -529,11 +529,9 @@
         x_hat, scale = normalise(tok[at, :].astype(F32))
         add_rows(sg, plan["gain1"][0], total(grad * x_hat))
         add_rows(sg, plan["shift1"][0], total(grad))
-        norm[at, :] = (t3[at, :] + norm_back(x_hat, scale, grad * gain1[...][None, :])).astype(BF16)
+        ing_ref[at, :] = (t3[at, :] + norm_back(x_hat, scale, grad * gain1[...][None, :])).astype(BF16)
 
     each(first_norm_back)
-    to_ing = pltpu.make_async_copy(norm, ing_h, lsem.at[1])
-    to_ing.start()
 
     rows = plan["genes"][1]
     local = genes[...][None, :] - core * plan["genes"][2]
@@ -548,9 +546,8 @@
         small.tick(i)
         return carry
 
-    left = g.shape[0] + big.stages - tau
+    left = big.chunks + big.stages - tau
     lax.fori_loop(0, max(left, small.stages + 1), finish, 0)
-    to_ing.wait()
 
 
 def run_layer(n_dp, plan, small_rows, *args):
@@ -567,13 +564,13 @@
     return pl.pallas_call(
         functools.partial(layer, n_dp, plan),
         out_shape=(
-            jax.ShapeDtypeStruct(wide, BF16),
-            jax.ShapeDtypeStruct(wide, BF16),
-            jax.ShapeDtypeStruct((chunks, PARTS, BLK, BLK), F32),
-            jax.ShapeDtypeStruct((1, 1, small_rows, LANES), F32),
+            pltpu.VMEM(wide, BF16),
+            pltpu.VMEM(wide, BF16),
+            pltpu.VMEM((chunks, PARTS, BLK, BLK), F32),
+            pltpu.VMEM((1, 1, small_rows, LANES), F32),
         ),
         in_specs=[smem, vmem, hbm, hbm, vmem, vmem, hbm, vmem, hbm, vmem, vmem, vmem, hbm, vmem, hbm, vmem],
-        out_specs=(hbm, hbm, hbm, hbm),
+        out_specs=(vmem, vmem, vmem, vmem),
         scratch_shapes=[
             pltpu.VMEM(wide, BF16),
             pltpu.VMEM(wide, BF16),
@@ -581,27 +578,21 @@
             pltpu.VMEM(outw.shape, BF16),
             pltpu.VMEM(upw.shape, BF16),
             pltpu.VMEM(dnw.shape, BF16),
-            pltpu.VMEM(wide, BF16),
             pltpu.VMEM((features, tokens), BF16),
             pltpu.VMEM((tokens, head_cols), BF16),
             pltpu.VMEM((tokens, head_cols), BF16),
             pltpu.VMEM((tokens, head_cols), BF16),
-            pltpu.VMEM((head_cols, tokens), BF16),
             pltpu.VMEM((tokens, head_cols), BF16),
-            pltpu.VMEM((tokens, head_cols), BF16),
-            pltpu.VMEM((head_cols, tokens), BF16),
             pltpu.VMEM(wide, F32),
             pltpu.VMEM(wide, F32),
             pltpu.VMEM(wide, F32),
             pltpu.VMEM(wide, F32),
-            pltpu.VMEM((chunks, PARTS, BLK, BLK), F32),
+            pltpu.VMEM((HELD, PARTS, BLK, BLK), F32),
             pltpu.VMEM((SLOTS, PARTS, slot_rows(n_dp, BLK), BLK), F32),
             pltpu.VMEM((tokens, BLK), BF16),
             pltpu.VMEM((BLK, tokens), BF16),
             pltpu.VMEM((tokens, BLK), BF16),
             pltpu.VMEM((tokens, BLK), F32),
-            pltpu.VMEM((tokens, LANES), F32),
-            pltpu.VMEM((tokens, LANES), F32),
             pltpu.VMEM((tokens, LANES), jnp.int32),
             pltpu.VMEM((1, 1, small_rows, LANES), F32),
             pltpu.VMEM((1, 1, slot_rows(n_dp, small_rows), LANES), F32),
@@ -617,52 +608,40 @@
             pltpu.SemaphoreType.REGULAR,
         ],
         compiler_params=pltpu.CompilerParams(
-            collective_id=0, has_side_effects=True, vmem_limit_bytes=63 << 20
+            collective_id=0, has_side_effects=True, vmem_limit_bytes=47 << 20
         ),
     )(*args)
 
 
-def hand_out(plan, packed_h, sums, out_h, ing_h, *refs):
+def hand_out(plan, packed, sums, out_ref, ing_ref, *refs):
     (output, input_grad, gain1, shift1, qkv, qv, out, obias, gain2, shift2, up, ubias, down, dbias, genes) = refs[:15]
-    packed, wide, loaded, sem = refs[15:]
-    chunks = packed.shape[0]
-    loads = [pltpu.make_async_copy(packed_h.at[c], packed.at[c], loaded.at[c]) for c in range(chunks)]
-    loads.append(pltpu.make_async_copy(out_h, wide.at[0], loaded.at[chunks]))
-    loads.append(pltpu.make_async_copy(ing_h, wide.at[1], loaded.at[chunks + 1]))
-    for load in loads:
-        load.start()
-    moves = [[] for load in loads]
-    moves[chunks].append((wide.at[0], output))
-    moves[chunks + 1].append((wide.at[1], input_grad))
+    sem = refs[15]
+    moves = [(out_ref, output), (ing_ref, input_grad)]
     for u in range(down.shape[0] // BLK):
         for p in range(PARTS):
             units, cols = pl.ds(u * BLK, BLK), pl.ds(p * BLK, BLK)
-            moves[2 * u].append((packed.at[2 * u, p], down.at[units, cols]))
-            moves[2 * u + 1].append((packed.at[2 * u + 1, p], up.at[cols, units]))
+            moves.append((packed.at[2 * u, p], down.at[units, cols]))
+            moves.append((packed.at[2 * u + 1, p], up.at[cols, units]))
     half = pl.ds(0, LANES), pl.ds(LANES, LANES)
     for p in range(PARTS):
         cols = pl.ds(p * BLK, BLK)
-        moves[12].append((packed.at[12, p], out.at[pl.ds(0, BLK), cols]))
-        rest = packed.at[17, 1 + p // 2, half[p % 2]]
-        moves[17].append((rest, out.at[pl.ds(BLK, LANES), cols]))
+        moves.append((packed.at[12, p], out.at[pl.ds(0, BLK), cols]))
+        rest = packed.at[13, 1 + p // 2, half[p % 2]]
+        moves.append((rest, out.at[pl.ds(BLK, LANES), cols]))
     for i in range(3):
         for j in range(PARTS):
             rows, tail = pl.ds(j * BLK, BLK), pl.ds(BLK, LANES)
-            moves[13 + i].append((packed.at[13 + i, j], qkv.at[i, rows, pl.ds(0, BLK)]))
+            moves.append((packed.at[14 + i, j], qkv.at[i, rows, pl.ds(0, BLK)]))
             if i * 3 + j < 8:
                 c, p, side = leftover(i * 3 + j)
-                moves[c].append((packed.at[c, p, pl.ds(0, BLK), half[side]], qkv.at[i, rows, tail]))
+                moves.append((packed.at[c, p, pl.ds(0, BLK), half[side]], qkv.at[i, rows, tail]))
             else:
                 for side in range(2):
                     rows = pl.ds(j * BLK + side * LANES, LANES)
-                    moves[17].append((packed.at[17, 2, half[1], half[side]], qkv.at[i, rows, tail]))
-    copies = []
-    for load, group in zip(loads, moves):
-        load.wait()
-        for src, dst in group:
-            copy = pltpu.make_async_copy(src, dst, sem.at[len(copies)])
-            copy.start()
-            copies.append(copy)
+                    moves.append((packed.at[13, 2, half[1], half[side]], qkv.at[i, rows, tail]))
+    copies = [pltpu.make_async_copy(src, dst, sem.at[i]) for i, (src, dst) in enumerate(moves)]
+    for copy in copies:
+        copy.start()
 
     def vector(name, ref, *index):
         at, count, _ = plan[name]
@@ -715,15 +694,12 @@
     return pl.pallas_call(
         functools.partial(hand_out, plan),
         out_shape=tuple(jax.ShapeDtypeStruct(shape, kind) for shape, kind in zip(shapes, types)),
-        in_specs=[hbm, vmem, hbm, hbm],
+        in_specs=[vmem, vmem, vmem, vmem],
         out_specs=tuple(hbm if i in large else vmem for i in range(15)),
         scratch_shapes=[
-            pltpu.VMEM(packed.shape, F32),
-            pltpu.VMEM((2, *output.shape), BF16),
-            pltpu.SemaphoreType.DMA((packed.shape[0] + 2,)),
             pltpu.SemaphoreType.DMA((80,)),
         ],
-        compiler_params=pltpu.CompilerParams(vmem_limit_bytes=60 << 20),
+        compiler_params=pltpu.CompilerParams(vmem_limit_bytes=16 << 20),
     )(packed, sums, output, input_grad)
 
 

time: 260 us -> 251 us (0.965)
  Pallas kernels: 259 us -> 250 us
    pallas_call x1, Pallas kernels: 14.4 us -> 7.3 us  [results(): pl.pallas_call(functools.partial(hand_out, plan), out_shape=tuple((jax.Sh...]
where the time goes in v4:
time: 251 us
  Pallas kernels  250 us (100%)
    pallas_call x1, Pallas kernels, run_layer(): pl.pallas_call(functools.partial(layer, n_dp, plan), out_shape=(pltpu.VME...  243 us
    pallas_call x1, Pallas kernels, results(): pl.pallas_call(functools.partial(hand_out, plan), out_shape=tuple((jax.Sh...  7.3 us

profile of v4, /device:TPU:0, one launch (start us, length us, event | category | flops | bytes accessed | tf_op | source)
XLA Modules:
  0.0 251.3 jit_solution(14183721913559341706)
XLA Ops:
  0.7 243.2 %shard_map.271 = (bf16[1024,768]{1,0:T(8,128)(2,1)S(1)}, bf16[1024,768]{1,0:T(8,128)(2,1)S(1)}, f32[18,3,256,256]{3,2,1,0:T(8,128)S(1)}, f32[1,1,256,128]{3,2,1,0:T(8,128)S(1)}) custom-call(s32[1,6]{1,0:T(1,128)} %lengths.1, s32[1024]{0:T(1024)} %genes.1, bf16[1024,768]{1,0:T(8,128)(2,1)} %tok_h.1, bf16[1024,768]{1,0:T(8,128)(2,1)} %cot_h.1, f32[768]{0:T(1024)} %gain1.1, ...), custom_call_target="tpu_custom_call" | custom-call | tf_op jit(solution)/shard_map/pallas_call | solution.py:564
  243.8 7.3 %shard_map.272 = (bf16[1024,768]{1,0:T(8,128)(2,1)}, bf16[1024,768]{1,0:T(8,128)(2,1)}, f32[768]{0:T(1024)}, f32[768]{0:T(1024)}, f32[3,768,384]{2,1,0:T(8,128)}...) custom-call(f32[18,3,256,256]{3,2,1,0:T(8,128)S(1)} %get-tuple-eleme, ...), custom_call_target="tpu_custom_call" | custom-call | tf_op jit(solution)/shard_map/pallas_call | solution.py:694

commit v5 on v4

--- a/solution.py
+++ b/solution.py
@@ -91,15 +91,15 @@
         return pltpu.make_async_remote_copy(
             src,
             dst,
-            self.ssem.at[c, p, s],
-            self.rsem.at[c, p, s],
+            self.ssem.at[lax.rem(c, self.slots), p, s],
+            self.rsem.at[lax.rem(c, self.slots), p, s],
             device_id=(self.dp + mask * (1 - 2 * bit), self.core),
             device_id_type=MESH,
         )
 
     def keep(self, c, p):
         mine = self.own(c, p, self.half)
-        return pltpu.make_async_copy(self.g.at[self.held(c), p, mine], self.o.at[c, p, mine], self.osem.at[c, p])
+        return pltpu.make_async_copy(self.g.at[self.held(c), p, mine], self.o.at[c, p, mine], self.osem.at[lax.rem(c, self.slots), p])
 
     def tick(self, tau):
         flat_end = self.stages - self.half
@@ -192,22 +192,22 @@
 def layer(
     n_dp,
     plan,
-    lengths,
-    genes,
+    lengths_h,
+    genes_h,
     tok_h,
     cot_h,
-    gain1,
-    shift1,
+    gain1_h,
+    shift1_h,
     qkvw_h,
-    qvb,
+    qvb_h,
     outw_h,
-    obias,
-    gain2,
-    shift2,
+    obias_h,
+    gain2_h,
+    shift2_h,
     upw_h,
-    ubias,
+    ubias_h,
     dnw_h,
-    dbias,
+    dbias_h,
     out_ref,
     ing_ref,
     o,
@@ -232,7 +232,6 @@
     act,
     act_t,
     gu,
-    slope,
     seg,
     sg,
     sr,
@@ -246,6 +245,16 @@
     srsem,
     sosem,
     vfree,
+    lengths,
+    genes,
+    gain1,
+    shift1,
+    qvb,
+    obias,
+    gain2,
+    shift2,
+    ubias,
+    dbias,
 ):
     tokens, features = tok.shape
     head_cols = qs.shape[1]
@@ -253,14 +262,31 @@
     rbs = tokens // BLK
     dq_t, x_t = norm_t.at[:head_cols], norm_t.at[head_cols : 2 * head_cols]
     dctx, norm = ctx, ing_ref
-    dk_sum, dv_sum = slope.at[:, :LANES], slope.at[:, LANES:]
+    slope, dk_sum, dv_sum = v.at[:, :BLK], v.at[:, :LANES], v.at[:, LANES:BLK]
     dp, core = lax.axis_index("dp"), lax.axis_index("tensor")
     other = (dp, 1 - core)
 
     loads = [
         pltpu.make_async_copy(src, dst, lsem.at[i])
         for i, (src, dst) in enumerate(
-            ((tok_h, tok), (qkvw_h, qkvw), (outw_h, outw), (upw_h, upw), (cot_h, cot), (dnw_h, dnw))
+            (
+                (tok_h, tok),
+                (lengths_h, lengths),
+                (gain1_h, gain1),
+                (shift1_h, shift1),
+                (qkvw_h, qkvw),
+                (qvb_h, qvb),
+                (outw_h, outw),
+                (obias_h, obias),
+                (gain2_h, gain2),
+                (shift2_h, shift2),
+                (upw_h, upw),
+                (ubias_h, ubias),
+                (cot_h, cot),
+                (dnw_h, dnw),
+                (dbias_h, dbias),
+                (genes_h, genes),
+            )
         )
     ]
     for load in loads:
@@ -300,10 +326,12 @@
             seg_now = seg_now + (position >= ends).astype(jnp.int32)
         return seg_now
 
+    loads[1].wait()
     seg[...] = segment(lax.broadcasted_iota(jnp.int32, (tokens, LANES), 0))
     sg[...] = jnp.zeros_like(sg)
 
-    loads[0].wait()
+    for i in (0, 2, 3):
+        loads[i].wait()
 
     def first_norm(rb):
         at = rows_at(rb, BLK)
@@ -311,7 +339,8 @@
         norm[at, :] = (x_hat * gain1[...][None, :] + shift1[...][None, :]).astype(BF16)
 
     each(first_norm)
-    loads[1].wait()
+    for load in loads[4:6]:
+        load.wait()
 
     def project(rb):
         at = rows_at(rb, BLK)
@@ -321,7 +350,7 @@
         vs[at, :] = (mm(x, qkvw[2]) + qvb[1:2, :]).astype(BF16)
 
     each(project)
-    loads[2].wait()
+    loads[6].wait()
     pl.semaphore_wait(bar, bits + 1)
 
     def attend(rb):
@@ -335,15 +364,14 @@
                 scores = jnp.where(same, mm_t(qs[at, cols], ks[:, cols]), -1000000000.0)
                 e = jnp.exp(scores - jnp.max(scores, axis=-1, keepdims=True))
                 inverse = 1.0 / jnp.sum(e, axis=-1, keepdims=True)
-                sides.append(mm((e * inverse).astype(BF16), vs[:, cols]))
+                sides.append(mm(e.astype(BF16), vs[:, cols]) * inverse)
             ctx[at, pair * LANES : (pair + 1) * LANES] = jnp.concatenate(sides, axis=1).astype(BF16)
         t1[at, :] = mm(ctx[at, :], outw[...])
         swap(0, t1, rb).start()
 
     each(attend)
-    loads[3].wait()
-    loads[4].wait()
-    loads[5].wait()
+    for load in loads[7:]:
+        load.wait()
 
     def second_norm(rb):
         at = rows_at(rb, BLK)
@@ -356,7 +384,6 @@
         t3[at, :] = jnp.zeros((BLK, features), F32)
 
     each(second_norm)
-    freed()
 
     def feed_forward(u):
         ucols = rows_at(u, BLK)
@@ -399,6 +426,7 @@
             big.tick(1)
 
     each(feed_forward, units // BLK)
+    freed()
     tau = units // BLK + 1
 
     pl.semaphore_wait(vfree, 1)
@@ -445,7 +473,6 @@
         out_ref[at, :] = (t1[at, :] + (t2[at, :] + v[at, :]) + dbias[...][None, :]).astype(BF16)
 
     each(result)
-    freed()
 
     x_t[...] = ks[...].T
 
@@ -493,6 +520,7 @@
 
     steps = rbs * (head_cols // LANES)
     each(attend_back, steps)
+    freed()
     tau += steps // 3
 
     qs[...] = dq_t[...].T
@@ -557,7 +585,6 @@
     chunks = (features * (2 * units + 4 * head_cols)) // (PARTS * BLK * BLK)
     _, _, stages = stage_counts(n_dp)
     vmem = pl.BlockSpec(memory_space=pltpu.VMEM)
-    smem = pl.BlockSpec(memory_space=pltpu.SMEM)
     hbm = pl.BlockSpec(memory_space=pl.ANY)
     dma = pltpu.SemaphoreType.DMA
     wide = (tokens, features)
@@ -569,7 +596,7 @@
             pltpu.VMEM((chunks, PARTS, BLK, BLK), F32),
             pltpu.VMEM((1, 1, small_rows, LANES), F32),
         ),
-        in_specs=[smem, vmem, hbm, hbm, vmem, vmem, hbm, vmem, hbm, vmem, vmem, vmem, hbm, vmem, hbm, vmem],
+        in_specs=[hbm] * 16,
         out_specs=(vmem, vmem, vmem, vmem),
         scratch_shapes=[
             pltpu.VMEM(wide, BF16),
@@ -592,20 +619,22 @@
             pltpu.VMEM((tokens, BLK), BF16),
             pltpu.VMEM((BLK, tokens), BF16),
             pltpu.VMEM((tokens, BLK), BF16),
-            pltpu.VMEM((tokens, BLK), F32),
             pltpu.VMEM((tokens, LANES), jnp.int32),
             pltpu.VMEM((1, 1, small_rows, LANES), F32),
             pltpu.VMEM((1, 1, slot_rows(n_dp, small_rows), LANES), F32),
-            dma((6,)),
+            dma((16,)),
             dma((4, tokens // BLK)),
             dma((4, tokens // BLK)),
-            dma((chunks, PARTS, stages)),
-            dma((chunks, PARTS, stages)),
-            dma((chunks, PARTS)),
+            dma((SLOTS, PARTS, stages)),
+            dma((SLOTS, PARTS, stages)),
+            dma((SLOTS, PARTS)),
             dma((1, 1, stages)),
             dma((1, 1, stages)),
             dma((1, 1)),
             pltpu.SemaphoreType.REGULAR,
+            pltpu.SMEM(lengths.shape, jnp.int32),
+            pltpu.VMEM(genes.shape, jnp.int32),
+            *(pltpu.VMEM(x.shape, F32) for x in (gain1, shift1, qvb, obias, gain2, shift2, ubias, dbias)),
         ],
         compiler_params=pltpu.CompilerParams(
             collective_id=0, has_side_effects=True, vmem_limit_bytes=47 << 20

time: 251 us -> 243 us (0.968)
  Pallas kernels: 250 us -> 242 us
    pallas_call x1, Pallas kernels: 243 us -> 234 us  [run_layer(): pl.pallas_call(functools.partial(layer, n_dp, plan), out_shape=(pltpu.VME...]
where the time goes in v5:
time: 243 us; the launch traced here: 242 us
  Pallas kernels  242 us (100%)
    pallas_call x1, Pallas kernels, run_layer(): pl.pallas_call(functools.partial(layer, n_dp, plan), out_shape=(pltpu.VME...  234 us
    pallas_call x1, Pallas kernels, results(): pl.pallas_call(functools.partial(hand_out, plan), out_shape=tuple((jax.Sh...  7.3 us

profile of v5, /device:TPU:0, one launch (start us, length us, event | category | flops | bytes accessed | tf_op | source)
XLA Modules:
  0.0 242.4 jit_solution(17068843223829525577)
XLA Ops:
  0.7 234.3 %shard_map.271 = (bf16[1024,768]{1,0:T(8,128)(2,1)S(1)}, bf16[1024,768]{1,0:T(8,128)(2,1)S(1)}, f32[18,3,256,256]{3,2,1,0:T(8,128)S(1)}, f32[1,1,256,128]{3,2,1,0:T(8,128)S(1)}) custom-call(s32[1,6]{1,0:T(1,128)} %lengths_h.1, s32[1024]{0:T(1024)} %genes_h.1, bf16[1024,768]{1,0:T(8,128)(2,1)} %tok_h.1, bf16[1024,768]{1,0:T(8,128)(2,1)} %cot_h.1, ...), custom_call_target="tpu_custom_call" | custom-call | tf_op jit(solution)/shard_map/pallas_call | solution.py:591
  234.9 7.3 %shard_map.272 = (bf16[1024,768]{1,0:T(8,128)(2,1)}, bf16[1024,768]{1,0:T(8,128)(2,1)}, f32[768]{0:T(1024)}, f32[768]{0:T(1024)}, f32[3,768,384]{2,1,0:T(8,128)}...) custom-call(f32[18,3,256,256]{3,2,1,0:T(8,128)S(1)} %get-tuple-eleme, ...), custom_call_target="tpu_custom_call" | custom-call | tf_op jit(solution)/shard_map/pallas_call | solution.py:723

commit v6 on v5

--- a/solution.py
+++ b/solution.py
@@ -91,7 +91,7 @@
         return pltpu.make_async_remote_copy(
             src,
             dst,
-            self.ssem.at[lax.rem(c, self.slots), p, s],
+            self.ssem.at[lax.rem(c, self.ssem.shape[0]), p, s],
             self.rsem.at[lax.rem(c, self.slots), p, s],
             device_id=(self.dp + mask * (1 - 2 * bit), self.core),
             device_id_type=MESH,
@@ -99,7 +99,7 @@
 
     def keep(self, c, p):
         mine = self.own(c, p, self.half)
-        return pltpu.make_async_copy(self.g.at[self.held(c), p, mine], self.o.at[c, p, mine], self.osem.at[lax.rem(c, self.slots), p])
+        return pltpu.make_async_copy(self.g.at[self.held(c), p, mine], self.o.at[c, p, mine], self.osem.at[lax.rem(c, self.osem.shape[0]), p])
 
     def tick(self, tau):
         flat_end = self.stages - self.half
@@ -229,9 +229,7 @@
     v,
     g,
     r,
-    act,
     act_t,
-    gu,
     seg,
     sg,
     sr,
@@ -262,6 +260,7 @@
     rbs = tokens // BLK
     dq_t, x_t = norm_t.at[:head_cols], norm_t.at[head_cols : 2 * head_cols]
     dctx, norm = ctx, ing_ref
+    act, gu = out_ref.at[:, :BLK], out_ref.at[:, BLK : 2 * BLK]
     slope, dk_sum, dv_sum = v.at[:, :BLK], v.at[:, :LANES], v.at[:, LANES:BLK]
     dp, core = lax.axis_index("dp"), lax.axis_index("tensor")
     other = (dp, 1 - core)
@@ -357,15 +356,23 @@
         at = rows_at(rb, BLK)
         seg_row = segment(lax.broadcasted_iota(jnp.int32, (1, tokens), 1))
         same = jnp.concatenate([seg[at, :]] * (tokens // LANES), axis=1) == seg_row
-        for pair in range(head_cols // LANES):
-            sides = []
-            for side in range(2):
-                cols = slice(pair * LANES + side * HEAD, pair * LANES + (side + 1) * HEAD)
-                scores = jnp.where(same, mm_t(qs[at, cols], ks[:, cols]), -1000000000.0)
-                e = jnp.exp(scores - jnp.max(scores, axis=-1, keepdims=True))
-                inverse = 1.0 / jnp.sum(e, axis=-1, keepdims=True)
-                sides.append(mm(e.astype(BF16), vs[:, cols]) * inverse)
-            ctx[at, pair * LANES : (pair + 1) * LANES] = jnp.concatenate(sides, axis=1).astype(BF16)
+        heads = head_cols // HEAD
+
+        def scores_of(h):
+            cols = slice(h * HEAD, (h + 1) * HEAD)
+            return jnp.where(same, mm_t(qs[at, cols], ks[:, cols]), -1000000000.0)
+
+        ready, sides = scores_of(0), []
+        for h in range(heads):
+            scores = ready
+            if h + 1 < heads:
+                ready = scores_of(h + 1)
+            e = jnp.exp(scores - jnp.max(scores, axis=-1, keepdims=True))
+            inverse = 1.0 / jnp.sum(e, axis=-1, keepdims=True)
+            sides.append(mm(e.astype(BF16), vs[:, h * HEAD : (h + 1) * HEAD]) * inverse)
+            if h % 2:
+                ctx[at, (h - 1) * HEAD : (h + 1) * HEAD] = jnp.concatenate(sides, axis=1).astype(BF16)
+                sides = []
         t1[at, :] = mm(ctx[at, :], outw[...])
         swap(0, t1, rb).start()
 
@@ -616,18 +623,16 @@
             pltpu.VMEM(wide, F32),
             pltpu.VMEM((HELD, PARTS, BLK, BLK), F32),
             pltpu.VMEM((SLOTS, PARTS, slot_rows(n_dp, BLK), BLK), F32),
-            pltpu.VMEM((tokens, BLK), BF16),
             pltpu.VMEM((BLK, tokens), BF16),
-            pltpu.VMEM((tokens, BLK), BF16),
             pltpu.VMEM((tokens, LANES), jnp.int32),
             pltpu.VMEM((1, 1, small_rows, LANES), F32),
             pltpu.VMEM((1, 1, slot_rows(n_dp, small_rows), LANES), F32),
             dma((16,)),
             dma((4, tokens // BLK)),
             dma((4, tokens // BLK)),
+            dma((2, PARTS, stages)),
             dma((SLOTS, PARTS, stages)),
-            dma((SLOTS, PARTS, stages)),
-            dma((SLOTS, PARTS)),
+            dma((2, PARTS)),
             dma((1, 1, stages)),
             dma((1, 1, stages)),
             dma((1, 1)),
@@ -726,7 +731,7 @@
         in_specs=[vmem, vmem, vmem, vmem],
         out_specs=tuple(hbm if i in large else vmem for i in range(15)),
         scratch_shapes=[
-            pltpu.SemaphoreType.DMA((80,)),
+            pltpu.SemaphoreType.DMA((63,)),
         ],
         compiler_params=pltpu.CompilerParams(vmem_limit_bytes=16 << 20),
     )(packed, sums, output, input_grad)

time: 243 us -> 239 us (0.984)
  Pallas kernels: 242 us -> 238 us
    pallas_call x1, Pallas kernels: 234 us -> 231 us  [run_layer(): pl.pallas_call(functools.partial(layer, n_dp, plan), out_shape=(pltpu.VME...]
where the time goes in v6:
time: 239 us
  Pallas kernels  238 us (100%)
    pallas_call x1, Pallas kernels, run_layer(): pl.pallas_call(functools.partial(layer, n_dp, plan), out_shape=(pltpu.VME...  231 us
    pallas_call x1, Pallas kernels, results(): pl.pallas_call(functools.partial(hand_out, plan), out_shape=tuple((jax.Sh...  7.15 us

profile of v6, /device:TPU:0, one launch (start us, length us, event | category | flops | bytes accessed | tf_op | source)
XLA Modules:
  0.0 239.3 jit_solution(7617385243038747404)
XLA Ops:
  0.7 231.3 %shard_map.271 = (bf16[1024,768]{1,0:T(8,128)(2,1)S(1)}, bf16[1024,768]{1,0:T(8,128)(2,1)S(1)}, f32[18,3,256,256]{3,2,1,0:T(8,128)S(1)}, f32[1,1,256,128]{3,2,1,0:T(8,128)S(1)}) custom-call(s32[1,6]{1,0:T(1,128)} %lengths_h.1, s32[1024]{0:T(1024)} %genes_h.1, bf16[1024,768]{1,0:T(8,128)(2,1)} %tok_h.1, bf16[1024,768]{1,0:T(8,128)(2,1)} %cot_h.1, ...), custom_call_target="tpu_custom_call" | custom-call | tf_op jit(solution)/shard_map/pallas_call | solution.py:598
  232.0 7.1 %shard_map.272 = (bf16[1024,768]{1,0:T(8,128)(2,1)}, bf16[1024,768]{1,0:T(8,128)(2,1)}, f32[768]{0:T(1024)}, f32[768]{0:T(1024)}, f32[3,768,384]{2,1,0:T(8,128)}...) custom-call(f32[18,3,256,256]{3,2,1,0:T(8,128)S(1)} %get-tuple-eleme, ...), custom_call_target="tpu_custom_call" | custom-call | tf_op jit(solution)/shard_map/pallas_call | solution.py:728

commit v7 on v6

--- a/solution.py
+++ b/solution.py
@@ -647,9 +647,13 @@
     )(*args)
 
 
+SMALL = (2, 3, 5, 7, 8, 9, 11, 13, 14)
+
+
 def hand_out(plan, packed, sums, out_ref, ing_ref, *refs):
-    (output, input_grad, gain1, shift1, qkv, qv, out, obias, gain2, shift2, up, ubias, down, dbias, genes) = refs[:15]
-    sem = refs[15]
+    output, input_grad, _, _, qkv, _, out, _, _, _, up, _, down, _, _ = refs[:15]
+    sem, *staged = refs[15:]
+    gain1, shift1, qv, obias, gain2, shift2, ubias, dbias, genes = staged
     moves = [(out_ref, output), (ing_ref, input_grad)]
     for u in range(down.shape[0] // BLK):
         for p in range(PARTS):
@@ -698,6 +702,9 @@
     for i in range(-(-size // LANES)):
         part = min(LANES, size - i * LANES)
         genes[pl.ds(i * LANES, part)] = sums[0, 0, i, :part].astype(jnp.int32)
+    for src, at in zip(staged, SMALL):
+        copies.append(pltpu.make_async_copy(src, refs[at], sem.at[len(copies)]))
+        copies[-1].start()
     for copy in copies:
         copy.wait()
 
@@ -724,14 +731,14 @@
         size("genes"),
     )
     types = [BF16, BF16] + [F32] * 12 + [jnp.int32]
-    large = (0, 1, 4, 6, 10, 12)
     return pl.pallas_call(
         functools.partial(hand_out, plan),
         out_shape=tuple(jax.ShapeDtypeStruct(shape, kind) for shape, kind in zip(shapes, types)),
         in_specs=[vmem, vmem, vmem, vmem],
-        out_specs=tuple(hbm if i in large else vmem for i in range(15)),
+        out_specs=(hbm,) * 15,
         scratch_shapes=[
-            pltpu.SemaphoreType.DMA((63,)),
+            pltpu.SemaphoreType.DMA((72,)),
+            *(pltpu.VMEM(shapes[i], types[i]) for i in SMALL),
         ],
         compiler_params=pltpu.CompilerParams(vmem_limit_bytes=16 << 20),
     )(packed, sums, output, input_grad)

time: 239 us -> 239 us (level)
  no operation moved by 1% of the time
where the time goes in v7:
time: 239 us
  Pallas kernels  238 us (100%)
    pallas_call x1, Pallas kernels, run_layer(): pl.pallas_call(functools.partial(layer, n_dp, plan), out_shape=(pltpu.VME...  231 us
    pallas_call x1, Pallas kernels, results(): pl.pallas_call(functools.partial(hand_out, plan), out_shape=tuple((jax.Sh...  6.61 us

profile of v7, /device:TPU:0, one launch (start us, length us, event | category | flops | bytes accessed | tf_op | source)
XLA Modules:
  0.0 238.8 jit_solution(5197038999798750073)
XLA Ops:
  0.7 231.3 %shard_map.271 = (bf16[1024,768]{1,0:T(8,128)(2,1)S(1)}, bf16[1024,768]{1,0:T(8,128)(2,1)S(1)}, f32[18,3,256,256]{3,2,1,0:T(8,128)S(1)}, f32[1,1,256,128]{3,2,1,0:T(8,128)S(1)}) custom-call(s32[1,6]{1,0:T(1,128)} %lengths_h.1, s32[1024]{0:T(1024)} %genes_h.1, bf16[1024,768]{1,0:T(8,128)(2,1)} %tok_h.1, bf16[1024,768]{1,0:T(8,128)(2,1)} %cot_h.1, ...), custom_call_target="tpu_custom_call" | custom-call | tf_op jit(solution)/shard_map/pallas_call | solution.py:598
  232.0 6.6 %shard_map.272 = (bf16[1024,768]{1,0:T(8,128)(2,1)}, bf16[1024,768]{1,0:T(8,128)(2,1)}, f32[768]{0:T(1024)}, f32[768]{0:T(1024)}, f32[3,768,384]{2,1,0:T(8,128)}...) custom-call(f32[18,3,256,256]{3,2,1,0:T(8,128)S(1)} %get-tuple-eleme, ...), custom_call_target="tpu_custom_call" | custom-call | tf_op jit(solution)/shard_map/pallas_call | solution.py:734

commit v8 on v7

--- a/solution.py
+++ b/solution.py
@@ -108,7 +108,7 @@
 
             @pl.when((c >= 0) & (c < self.chunks))
             def _():
-                for p in range(self.parts):
+                for p in (2, 0, 1) if self.parts == 3 else range(self.parts):
                     if s > 0:
                         self.copy(c, p, s - 1).wait()
                     if 0 < s <= flat_end:

time: 239 us -> 239 us (level)
  no operation moved by 1% of the time
where the time goes in v8:
time: 239 us
  Pallas kernels  238 us (100%)
    pallas_call x1, Pallas kernels, run_layer(): pl.pallas_call(functools.partial(layer, n_dp, plan), out_shape=(pltpu.VME...  231 us
    pallas_call x1, Pallas kernels, results(): pl.pallas_call(functools.partial(hand_out, plan), out_shape=tuple((jax.Sh...  6.61 us

profile of v8, /device:TPU:0, one launch (start us, length us, event | category | flops | bytes accessed | tf_op | source)
XLA Modules:
  0.0 238.8 jit_solution(4481772365764619707)
XLA Ops:
  0.7 231.4 %shard_map.271 = (bf16[1024,768]{1,0:T(8,128)(2,1)S(1)}, bf16[1024,768]{1,0:T(8,128)(2,1)S(1)}, f32[18,3,256,256]{3,2,1,0:T(8,128)S(1)}, f32[1,1,256,128]{3,2,1,0:T(8,128)S(1)}) custom-call(s32[1,6]{1,0:T(1,128)} %lengths_h.1, s32[1024]{0:T(1024)} %genes_h.1, bf16[1024,768]{1,0:T(8,128)(2,1)} %tok_h.1, bf16[1024,768]{1,0:T(8,128)(2,1)} %cot_h.1, ...), custom_call_target="tpu_custom_call" | custom-call | tf_op jit(solution)/shard_map/pallas_call | solution.py:598
  232.0 6.6 %shard_map.272 = (bf16[1024,768]{1,0:T(8,128)(2,1)}, bf16[1024,768]{1,0:T(8,128)(2,1)}, f32[768]{0:T(1024)}, f32[768]{0:T(1024)}, f32[3,768,384]{2,1,0:T(8,128)}...) custom-call(f32[18,3,256,256]{3,2,1,0:T(8,128)S(1)} %get-tuple-eleme, ...), custom_call_target="tpu_custom_call" | custom-call | tf_op jit(solution)/shard_map/pallas_call | solution.py:734
